TPU v7x, 32 devices: a whole 2x2x4 slice. The times are simulated.
32 devices in a mesh: dp: 16 (over z, y, core), shard: 2 (over x).
Axes of the slice: x: 2, y: 2, z: 4, core: 2. Of those that a mesh axis runs over, the one named last changes fastest.
Arguments:
- resid_in: bfloat16 [2048, 8192], P('dp', 'shard'), may hold values from -6 to 6
- hidden: bfloat16 [2048, 28672], P('shard', 'dp'), may hold values from -6 to 6
- w_down: bfloat16 [28672, 8192], P('dp', 'shard'), may hold values from -0.03125 to 0.03125
- frozen: bfloat16 [2048, 8192], P(('dp', 'shard')), may hold values from -6 to 6
- steer: bfloat16 [8192], P('shard'), may hold values from -6 to 6
- forget_flags: int32 [8], replicated, may hold values from 0 to 1, as said below
Outputs:
- updated: bfloat16 [2048, 8192], P('dp', 'shard')
- grad_down: float32 [28672, 8192], P('dp', 'shard')
Inputs may be any that keep to these rules, and one draw needn't show every extreme that they name: `forget_flags`: exactly half of the 8 sequences are forget sequences.
All inputs are finite; a program needn't handle non-finite values.
Results may differ from a plain program's by a relative error of at most 0.0019.
Values may be sent and summed in bfloat16 or wider, within the bound.
No kernel may reach another device: no remote copies, remote signals or barrier semaphores. Data moves between devices by JAX's collectives and lax.ppermute only.
A program may use at most 192 MiB of HBM per device.

v0:
```python
import math

import jax
import jax.numpy as jnp
from jax import lax
from jax.sharding import PartitionSpec as P

SEQ_LEN = 256


retain_weight = 2.0


def per_device(resid_in, hidden, w_down, frozen, steer, forget_flags):
    whole_hidden = lax.all_gather(hidden, "shard", axis=0, tiled=True)
    tok_rows = resid_in.shape[0]
    mlp_out = lax.psum_scatter(
        jnp.dot(whole_hidden, w_down, preferred_element_type=jnp.float32),
        "dp",
        scatter_dimension=0,
        tiled=True,
    )
    residual = resid_in.astype(jnp.float32) + mlp_out
    updated = residual.astype(jnp.bfloat16)
    target_rows = lax.all_to_all(frozen, "shard", split_axis=1, concat_axis=0, tiled=True)
    start_row = lax.axis_index("dp") * tok_rows
    seq_ids = (start_row + jnp.arange(tok_rows, dtype=jnp.int32)) // SEQ_LEN
    seq_match = seq_ids[:, None] == jnp.arange(forget_flags.shape[0], dtype=jnp.int32)[None, :]
    is_forget = jnp.sum(jnp.where(seq_match, forget_flags[None, :], 0), axis=1) > 0
    total_tokens = tok_rows * lax.axis_size("dp")
    target = jnp.where(
        is_forget[:, None], steer.astype(jnp.float32)[None, :], target_rows.astype(jnp.float32)
    )
    loss_weight = jnp.where(is_forget, 1.0, retain_weight).astype(jnp.float32)
    slopes = (loss_weight[:, None] * (residual - target) * (1.0 / math.sqrt(total_tokens))).astype(
        jnp.bfloat16
    )
    all_slopes = lax.all_gather(slopes, "dp", axis=0, tiled=True)
    grad_down = lax.dot_general(
        whole_hidden, all_slopes, (((0,), (0,)), ((), ())), preferred_element_type=jnp.float32
    )
    return (updated, grad_down)


def solution(mesh):
    in_specs = (
        P("dp", "shard"),
        P("shard", "dp"),
        P("dp", "shard"),
        P(("dp", "shard"), None),
        P("shard"),
        P(),
    )
    out_specs = (P("dp", "shard"), P("dp", "shard"))
    return jax.shard_map(
        per_device, mesh=mesh, in_specs=in_specs, out_specs=out_specs, check_vma=False
    )
```

profile of v0, /device:TPU:0, one launch (start us, length us, event | category | flops | bytes accessed | tf_op | source)
XLA Modules:
  0.0 680.7 jit_solution(4473470542726250037)
XLA Ops:
  7.2 0.0 all-gather.3.cloned.1.call-start
  7.2 0.7 all-gather.3.cloned.1.call-update
  7.9 0.0 reduce-scatter.2.cloned.1.call-start
  7.9 96.5 %all-gather.3.cloned.1.call-done = bf16[2048,1792]{1,0:T(8,128)(2,1)} async-done(((bf16[1024,1792]{1,0:T(8,128)(2,1)}), bf16[2048,1792]{1,0:T(8,128)(2,1)}) %all-gather.3.cloned.1.call-update) | async-done | bytes 7340048 | tf_op jit(solution)/shard_map/all_gather | solution.py:15
  104.5 38.7 %fusion.5 = f32[2048,4096]{1,0:T(8,128)} fusion(bf16[2048,1792]{1,0:T(8,128)(2,1)} %all-gather.3.cloned.1.call-done, bf16[1792,4096]{1,0:T(8,128)(2,1)} %param.8), kind=kOutput, calls=%fused_computation.17 | convolution fusion | flops 30064771072 | bytes 55574528 | tf_op jit(solution)/shard_map/dot_general | solution.py:18
  143.2 0.0 copy-start
  143.2 0.0 copy-start.2
  143.2 0.0 copy-start.3
  143.2 0.0 copy-start.1
  143.2 0.0 reduce-scatter.2.cloned.1.call-update
  143.2 1.2 copy-done
  144.4 1.0 copy.14
  145.4 3.6 all-to-all-start
  149.0 0.2 all-gather.5.cloned.1.call-start
  149.3 0.0 copy-done.2
  149.3 0.0 copy-done.3
  149.3 0.1 select_reduce_fusion
  149.4 13.5 %all-to-all-done = bf16[64,2,4096]{2,0,1:T(8,128)(2,1)S(1)} async-done(((bf16[64,2,4096]{2,0,1:T(8,128)(2,1)}), bf16[64,2,4096]{2,0,1:T(8,128)(2,1)S(1)}, u32[]{:S(2)}, u32[]{:S(2)}) %all-to-all-start) | async-done | bytes 1048608 | tf_op jit(solution)/shard_map/all_to_all | solution.py:25
  162.9 313.2 %reduce-scatter.2.cloned.1.call-done = f32[128,4096]{1,0:T(8,128)} async-done(((f32[2048,4096]{1,0:T(8,128)}), f32[128,4096]{1,0:T(8,128)}) %reduce-scatter.2.cloned.1.call-update) | async-done | bytes 2097168 | tf_op jit(solution)/shard_map/reduce_scatter | solution.py:17
  476.1 0.0 copy-done.1
  476.1 3.6 fusion.3
  479.7 0.0 all-gather.5.cloned.1.call-update
  479.7 126.1 %all-gather.5.cloned.1.call-done = bf16[2048,4096]{1,0:T(8,128)(2,1)} async-done(((bf16[128,4096]{1,0:T(8,128)(2,1)}), bf16[2048,4096]{1,0:T(8,128)(2,1)}) %all-gather.5.cloned.1.call-update) | async-done | bytes 16777232 | tf_op jit(solution)/shard_map/all_gather | solution.py:38
  605.8 39.0 %convolution_bitcast_fusion = f32[1792,4096]{0,1:T(8,128)} fusion(bf16[2048,4096]{1,0:T(8,128)(2,1)} %all-gather.5.cloned.1.call-done, bf16[2048,1792]{1,0:T(8,128)(2,1)} %all-gather.3.cloned.1.call-done), kind=kOutput, calls=%fused_computation | convolution fusion | flops 30064771072 | bytes 53477376 | tf_op jit(solution)/shard_map/dot_general | solution.py:39
  644.8 29.4 %copy.11 = f32[1792,4096]{1,0:T(8,128)} copy(f32[1792,4096]{0,1:T(8,128)} %convolution_bitcast_fusion) | data formatting | bytes 58720256
  (4 shorter events, 0.0 us)
Async XLA Ops:
  7.2 97.3 %all-gather.3.cloned.1.call-start = ((), (), s32[]{:S(2)}) async-start(), calls=%async_computation.2 | async-start | bytes 11010048 | tf_op jit(solution)/shard_map/all_gather | solution.py:15
  7.9 468.2 %reduce-scatter.2.cloned.1.call-start = ((), (), s32[]{:S(2)}) async-start(), calls=%async_computation.3 | async-start | bytes 35651584 | tf_op jit(solution)/shard_map/reduce_scatter | solution.py:17
  143.2 1.2 copy-start
  143.2 6.1 copy-start.2
  143.2 6.1 copy-start.3
  143.2 332.9 %copy-start.1 = (bf16[128,4096]{1,0:T(8,128)(2,1)S(1)}, bf16[128,4096]{1,0:T(8,128)(2,1)}, u32[]{:S(2)}) copy-start(bf16[128,4096]{1,0:T(8,128)(2,1)} %param.6) | copy-start | bytes 3145732
  145.4 17.4 %all-to-all-start = ((bf16[64,2,4096]{2,0,1:T(8,128)(2,1)}), bf16[64,2,4096]{2,0,1:T(8,128)(2,1)S(1)}, u32[]{:S(2)}, u32[]{:S(2)}) async-start(bf16[64,2,4096]{2,0,1:T(8,128)(2,1)} %bitcast.21), calls=%async_computation.1 | async-start | bytes 2097152 | tf_op jit(solution)/shard_map/all_to_all | solution.py:25
  149.0 456.7 %all-gather.5.cloned.1.call-start = ((), (), s32[]{:S(2)}) async-start(), calls=%async_computation.4 | async-start | bytes 17825792 | tf_op jit(solution)/shard_map/all_gather | solution.py:38
Sparse Core Ops, SparseCore 0:
  9.5 94.8 all-gather.2
  143.3 332.7 reduce-scatter.1
  479.8 125.9 all-gather.4
where the time goes:
time: 681 us
  waiting for transfers between devices  550 us (81%)
  matrix products  77.7 us (11%)
  local copies, waits for them, and re-layouts  31.7 us (5%)
  between operations  13.8 us (2%)
    reduce_scatter x1, waiting for transfers between devices, per_device(): lax.psum_scatter(jnp.dot(whole_hidden, w_down, preferred_element_type=jnp...  313 us
    all_gather x1, waiting for transfers between devices, per_device(): all_slopes = lax.all_gather(slopes, 'dp', axis=0, tiled=True)  126 us
    all_gather x1, waiting for transfers between devices, per_device(): whole_hidden = lax.all_gather(hidden, 'shard', axis=0, tiled=True)  96.5 us
    dot_general x1, matrix products, per_device(): lax.dot_general(whole_hidden, all_slopes, (((0,), (0,)), ((), ())), prefe...  39 us
    dot_general x1, matrix products, per_device(): jnp.dot(whole_hidden, w_down, preferred_element_type=jnp.float32)  38.7 us
    unnamed x9, local copies, waits for them, and re-layouts  30.6 us
  transfers between devices with their start and end apart: 4, of which 4 were waited for; matrix products, arithmetic and copies ran while one was open for 0% of the time, Pallas kernels for 0%

commit v1 on v0

v1 whole, which is shorter than its diff:
```python
import math

import jax
import jax.numpy as jnp
from jax import lax
from jax.experimental import pallas as pl
from jax.experimental.pallas import tpu as pltpu
from jax.sharding import PartitionSpec as P

SEQ_LEN = 256
RETAIN_WEIGHT = 2.0
F32, BF16, WIRE = jnp.float32, jnp.bfloat16, jnp.float16
VMEM_LIMIT = 56 * 1024 * 1024


def bits_of(count):
    return count.bit_length() - 1


def flip(array, axis, mask):
    return lax.ppermute(array, axis, [(i, i ^ mask) for i in range(lax.axis_size(axis))])


def slot_of(chip, nb):
    slot = 0
    for b in range(nb):
        slot = slot * 2 + ((chip >> b) & 1)
    return slot


def project(place, groups, w_down, nb):
    per, _, rows, units = groups[0].shape
    chips, feats = 2**nb, w_down.shape[1]
    block = min(1024, feats)

    def kernel(place_ref, *refs):
        group_refs, (w_ref, theirs_ref, mine_ref, rows_ref) = refs[: len(groups)], refs[len(groups) :]

        @pl.when(pl.program_id(0) == 0)
        def _():
            core, chip, shard = place_ref[0], place_ref[1], place_ref[2]
            for d, group_ref in enumerate(group_refs):
                for t in range(per):
                    slot = slot_of(chip ^ ((shard ^ d) * per + t), nb)
                    for parity in range(2):
                        rows_ref[core ^ parity, slot] = group_ref[t, parity]

        for parity, out_ref in ((1, theirs_ref), (0, mine_ref)):
            lhs = rows_ref[parity].reshape(chips * rows, units)
            out_ref[...] = jnp.dot(lhs, w_ref[...], preferred_element_type=F32)

    whole = [pl.BlockSpec(g.shape, lambda i, _: (0, 0, 0, 0)) for g in groups]
    column = pl.BlockSpec((chips * rows, block), lambda i, _: (0, i))
    partial = jax.ShapeDtypeStruct((chips * rows, feats), F32)
    return pl.pallas_call(
        kernel,
        grid_spec=pltpu.PrefetchScalarGridSpec(
            num_scalar_prefetch=1,
            grid=(feats // block,),
            in_specs=whole + [pl.BlockSpec((units, block), lambda i, _: (0, i))],
            out_specs=[column, column, pl.BlockSpec((2, chips, rows, units), lambda i, _: (0, 0, 0, 0))],
        ),
        out_shape=[partial, partial, jax.ShapeDtypeStruct((2, chips, rows, units), BF16)],
        compiler_params=pltpu.CompilerParams(vmem_limit_bytes=VMEM_LIMIT),
        cost_estimate=pl.CostEstimate(
            flops=4 * chips * rows * units * feats,
            bytes_accessed=2 * units * feats + 8 * chips * rows * feats + 8 * chips * rows * units,
            transcendentals=0,
        ),
    )(place, *groups, w_down)


def gradient(chunks, slopes, grad, start, feats):
    units, width = chunks[0].shape[3], slopes[0].shape[2]
    block = min(512, width)
    first = start // block

    def kernel(*refs):
        chunk_refs, slope_refs = refs[: len(chunks)], refs[len(chunks) : len(chunks) + 2]
        total, row = None, 0
        for ref in chunk_refs:
            _, chips, rows, _ = ref.shape
            for parity in range(2):
                term = lax.dot_general(
                    ref[parity].reshape(chips * rows, units),
                    slope_refs[parity][:, row : row + rows].reshape(chips * rows, block),
                    (((0,), (0,)), ((), ())),
                    preferred_element_type=F32,
                )
                total = term if total is None else total + term
            row += rows
        refs[-1][...] = total

    tokens = 2 * slopes[0].shape[0] * slopes[0].shape[1]
    in_specs = [pl.BlockSpec(c.shape, lambda i: (0, 0, 0, 0)) for c in chunks]
    in_specs += [pl.BlockSpec(s.shape[:2] + (block,), lambda i: (0, 0, i)) for s in slopes]
    args, alias = [*chunks, *slopes], {}
    if grad is not None:
        alias = {len(args): 0}
        args.append(grad)
        in_specs.append(pl.BlockSpec(memory_space=pl.ANY))
    return pl.pallas_call(
        kernel,
        grid=(width // block,),
        in_specs=in_specs,
        out_specs=pl.BlockSpec((units, block), lambda i: (0, first + i)),
        out_shape=jax.ShapeDtypeStruct((units, feats), F32),
        input_output_aliases=alias,
        compiler_params=pltpu.CompilerParams(vmem_limit_bytes=VMEM_LIMIT),
        cost_estimate=pl.CostEstimate(
            flops=2 * tokens * units * width,
            bytes_accessed=2 * tokens * (units + width) + 4 * units * width,
            transcendentals=0,
        ),
    )(*args)


def reduce_chips(total, order, nb):
    total = total.reshape((2,) * nb + total.shape[1:])
    left = list(range(nb))
    for b in order:
        at = left.index(b)
        sent = lax.index_in_dim(total, 1, at, keepdims=False).astype(WIRE)
        kept = lax.index_in_dim(total, 0, at, keepdims=False)
        total = kept.astype(F32) + flip(sent, "dp", 2 << b).astype(F32)
        left.remove(b)
    return total


def gather_chips(block, order, nb):
    have = []
    for b in order:
        have = sorted([*have, b])
        block = jnp.stack([block, flip(block, "dp", 2 << b)], axis=have.index(b))
    return block.reshape((2**nb,) + block.shape[nb:])


def per_device(resid_in, hidden, w_down, frozen, steer, forget_flags):
    n_dp, n_shard = lax.axis_size("dp"), lax.axis_size("shard")
    chips = n_dp // 2
    nb = bits_of(chips)
    tok_rows, feats = resid_in.shape
    units = hidden.shape[1]
    dp, shard = lax.axis_index("dp"), lax.axis_index("shard")
    core, chip = dp % 2, dp // 2
    place = jnp.stack([core, chip, shard]).astype(jnp.int32)
    spans = [tok_rows // 4] * 4
    quarters = 4

    own = hidden.reshape(chips // n_shard, 2, tok_rows, units)
    groups, row = [], 0
    for rows in spans:
        part = lax.slice_in_dim(own, row, row + rows, axis=2)
        groups.append([part] + [flip(part, "shard", d) for d in range(1, n_shard)])
        row += rows

    target_rows = lax.all_to_all(frozen, "shard", split_axis=1, concat_axis=0, tiled=True)
    seq = (dp * tok_rows + jnp.arange(tok_rows, dtype=jnp.int32)) // SEQ_LEN
    match = seq[:, None] == jnp.arange(forget_flags.shape[0], dtype=jnp.int32)[None, :]
    is_forget = jnp.sum(jnp.where(match, forget_flags[None, :], 0), axis=1, keepdims=True) > 0
    scale = jnp.where(is_forget, 1.0, RETAIN_WEIGHT).astype(F32) * (1.0 / math.sqrt(tok_rows * n_dp))
    target = jnp.where(is_forget, steer.astype(F32)[None, :], target_rows.astype(F32))

    updated, slopes, chunks, row = [], [], [], 0
    for k, rows in enumerate(spans):
        theirs, mine, chunk = project(place, groups[k], w_down, nb)
        chunks.append(chunk)
        total = (mine + flip(theirs, "dp", 1)).reshape(chips, rows, feats)
        order = list(range(nb))
        mlp_out = reduce_chips(total, order, nb)
        here = slice(row, row + rows)
        residual = resid_in[here].astype(F32) + mlp_out
        updated.append(residual.astype(BF16))
        slopes.append((scale[here] * (residual - target[here])).astype(BF16))
        row += rows
    updated = jnp.concatenate(updated)
    slopes = jnp.concatenate(slopes)

    grad, width = None, feats // quarters
    for q in range(quarters):
        order = list(reversed(range(nb)))
        mine = gather_chips(slopes[:, q * width : (q + 1) * width], order, nb)
        theirs = flip(mine, "dp", 1)
        grad = gradient(chunks, [mine, theirs], grad, q * width, feats)
    return updated, grad


def solution(mesh):
    in_specs = (
        P("dp", "shard"),
        P("shard", "dp"),
        P("dp", "shard"),
        P(("dp", "shard"), None),
        P("shard"),
        P(),
    )
    out_specs = (P("dp", "shard"), P("dp", "shard"))
    return jax.shard_map(
        per_device, mesh=mesh, in_specs=in_specs, out_specs=out_specs, check_vma=False
    )
```

time: 681 us -> 446 us (0.65)
  waiting for transfers between devices: 550 us -> 265 us
  Pallas kernels: 0 us -> 109 us
  matrix products: 77.7 us -> 0 us
  starting transfers between devices: 3.88 us -> 43.5 us
  local copies, waits for them, and re-layouts: 31.7 us -> 6.04 us
  other arithmetic: 3.67 us -> 21.2 us
  between operations: 13.8 us -> 1.1 us
    reduce_scatter x1 -> x0, waiting for transfers between devices: 313 us -> none  [per_device(): lax.psum_scatter(jnp.dot(whole_hidden, w_down, preferred_element_type=jnp...]
    ppermute x0 -> x36, waiting for transfers between devices: none -> 265 us  [flip(): lax.ppermute(array, axis, [(i, i ^ mask) for i in range(lax.axis_size(axi...]
    all_gather x2 -> x0, waiting for transfers between devices: 223 us -> none  [the longest x1 126 us: per_device(): all_slopes = lax.all_gather(slopes, 'dp', axis=0, tiled=True)]
    pallas_call x0 -> x8, Pallas kernels: none -> 109 us  [the longest x4 54.9 us: gradient(): pl.pallas_call(kernel, grid=(width // block,), in_specs=in_specs, out_spe...]
    dot_general x2 -> x0, matrix products: 77.7 us -> none  [the longest x1 39 us: per_device(): lax.dot_general(whole_hidden, all_slopes, (((0,), (0,)), ((), ())), prefe...]
    ppermute x0 -> x36, starting transfers between devices: none -> 40 us  [flip(): lax.ppermute(array, axis, [(i, i ^ mask) for i in range(lax.axis_size(axi...]
    unnamed x9 -> x28, local copies, waits for them, and re-layouts: 30.6 us -> 1.35 us
    add x0 -> x12, other arithmetic: none -> 13.7 us  [the longest x4 12.2 us: per_device(): total = (mine + flip(theirs, 'dp', 1)).reshape(chips, rows, feats)]
  transfers between devices with their start and end apart: 4 -> 37, of which waited for: 4 -> 21; matrix products, arithmetic and copies ran while one was open for 0% -> 5% of each run, Pallas kernels for 0% -> 21%
where the time goes in v1:
time: 446 us; the launch traced here: 445 us
  waiting for transfers between devices  265 us (59%)
  Pallas kernels  109 us (24%)
  starting transfers between devices  43.5 us (10%)
  other arithmetic  21.2 us (5%)
  local copies, waits for them, and re-layouts  6.04 us (1%)
    ppermute x36, waiting for transfers between devices, flip(): lax.ppermute(array, axis, [(i, i ^ mask) for i in range(lax.axis_size(axi...  265 us
    pallas_call x4, Pallas kernels, gradient(): pl.pallas_call(kernel, grid=(width // block,), in_specs=in_specs, out_spe...  54.9 us
    pallas_call x4, Pallas kernels, project(): pl.pallas_call(kernel, grid_spec=pltpu.PrefetchScalarGridSpec(num_scalar_...  53.6 us
    ppermute x36, starting transfers between devices, flip(): lax.ppermute(array, axis, [(i, i ^ mask) for i in range(lax.axis_size(axi...  40 us
    add x4, other arithmetic, per_device(): total = (mine + flip(theirs, 'dp', 1)).reshape(chips, rows, feats)  12.2 us
  transfers between devices with their start and end apart: 37, of which 21 were waited for; matrix products, arithmetic and copies ran while one was open for 5% of the time, Pallas kernels for 21%

profile of v1, /device:TPU:0, one launch (start us, length us, event | category | flops | bytes accessed | tf_op | source)
XLA Modules:
  0.0 445.2 jit_solution(1374058290408987871)
XLA Ops:
  0.6 3.3 fusion.40
  3.9 3.0 collective-permute-start.5
  7.6 20.6 %collective-permute-done.5.refs_1_ = bf16[4,2,32,1792]{3,2,1,0:T(8,128)(2,1)} collective-permute-done((bf16[4,2,32,1792]{3,2,1,0:T(8,128)(2,1)S(1)}, bf16[4,2,32,1792]{3,2,1,0:T(8,128)(2,1)}, u32[]{:S(2)}, u32[]{:S(2)}) %collective-permute-start.5) | collective-permute-done | bytes 917536 | tf_op jit(solution)/shard_map/ppermute | solution.py:21
  28.2 13.4 %shard_map.78 = (f32[256,4096]{1,0:T(8,128)}, f32[256,4096]{1,0:T(8,128)}, bf16[2,8,32,1792]{3,2,1,0:T(8,128)(2,1)}) custom-call(s32[3]{0:T(128)} %pad_add_fusion.place_ref, bf16[4,2,32,1792]{3,2,1,0:T(8,128)(2,1)} %copy-done.11, bf16[4,2,32,1792]{3,2,1,0:T(8,128)(2,1)} %collective-permute-done.5.refs_1_, bf16[1792,4096]{1,0:T(8,128)(2,1)} %refs_2_.7), custom_call_target="tpu_custom_call" | custom-call | flops 7516192768 | bytes 26738688 | tf_op jit(solution)/shard_map/pallas_call | solution.py:55
  42.7 3.6 all-to-all-start
  48.6 13.4 %shard_map.77 = (f32[256,4096]{1,0:T(8,128)}, f32[256,4096]{1,0:T(8,128)}, bf16[2,8,32,1792]{3,2,1,0:T(8,128)(2,1)}) custom-call(s32[3]{0:T(128)} %pad_add_fusion.place_ref, bf16[4,2,32,1792]{3,2,1,0:T(8,128)(2,1)} %get-tuple-element.34.refs_0_, bf16[4,2,32,1792]{3,2,1,0:T(8,128)(2,1)} %collective-permute-done.refs_1_, bf16[1792,4096]{1,0:T(8,128)(2,1)} %refs_2_.7), custom_call_target="tpu_custom_call" | custom-call | flops 7516192768 | bytes 26738688 | tf_op jit(solution)/shard_map/pallas_call | solution.py:55
  62.3 18.8 %collective-permute-done.10.refs_1_ = bf16[4,2,32,1792]{3,2,1,0:T(8,128)(2,1)} collective-permute-done((bf16[4,2,32,1792]{3,2,1,0:T(8,128)(2,1)S(1)}, bf16[4,2,32,1792]{3,2,1,0:T(8,128)(2,1)}, u32[]{:S(2)}, u32[]{:S(2)}) %collective-permute-start.10) | collective-permute-done | bytes 917536 | tf_op jit(solution)/shard_map/ppermute | solution.py:21
  81.1 13.4 %shard_map.79 = (f32[256,4096]{1,0:T(8,128)}, f32[256,4096]{1,0:T(8,128)}, bf16[2,8,32,1792]{3,2,1,0:T(8,128)(2,1)}) custom-call(s32[3]{0:T(128)} %pad_add_fusion.place_ref, bf16[4,2,32,1792]{3,2,1,0:T(8,128)(2,1)} %copy-done.10, bf16[4,2,32,1792]{3,2,1,0:T(8,128)(2,1)} %collective-permute-done.10.refs_1_, bf16[1792,4096]{1,0:T(8,128)(2,1)} %refs_2_.7), custom_call_target="tpu_custom_call" | custom-call | flops 7516192768 | bytes 26738688 | tf_op jit(solution)/shard_map/pallas_call | solution.py:55
  94.6 6.0 %collective-permute-done.15.refs_1_ = bf16[4,2,32,1792]{3,2,1,0:T(8,128)(2,1)} collective-permute-done((bf16[4,2,32,1792]{3,2,1,0:T(8,128)(2,1)S(1)}, bf16[4,2,32,1792]{3,2,1,0:T(8,128)(2,1)}, u32[]{:S(2)}, u32[]{:S(2)}) %collective-permute-start.15) | collective-permute-done | bytes 917536 | tf_op jit(solution)/shard_map/ppermute | solution.py:21
  100.6 13.4 %shard_map.80 = (f32[256,4096]{1,0:T(8,128)}, f32[256,4096]{1,0:T(8,128)}, bf16[2,8,32,1792]{3,2,1,0:T(8,128)(2,1)}) custom-call(s32[3]{0:T(128)} %pad_add_fusion.place_ref, bf16[4,2,32,1792]{3,2,1,0:T(8,128)(2,1)} %copy-done.9, bf16[4,2,32,1792]{3,2,1,0:T(8,128)(2,1)} %collective-permute-done.15.refs_1_, bf16[1792,4096]{1,0:T(8,128)(2,1)} %refs_2_.7), custom_call_target="tpu_custom_call" | custom-call | flops 7516192768 | bytes 26738688 | tf_op jit(solution)/shard_map/pallas_call | solution.py:55
  114.3 3.9 add.86
  120.4 2.8 add.81
  135.2 9.4 %collective-permute-done.7 = f16[2,2,32,4096]{3,2,1,0:T(8,128)(2,1)S(1)} collective-permute-done((f16[2,2,32,4096]{3,2,1,0:T(8,128)(2,1)S(1)}, f16[2,2,32,4096]{3,2,1,0:T(8,128)(2,1)S(1)}, u32[]{:S(2)}, u32[]{:S(2)}) %collective-permute-start.7) | collective-permute-done | bytes 1048608 | tf_op jit(solution)/shard_map/ppermute | solution.py:21
  146.8 20.3 %collective-permute-done.2 = f16[2,2,32,4096]{3,2,1,0:T(8,128)(2,1)S(1)} collective-permute-done((f16[2,2,32,4096]{3,2,1,0:T(8,128)(2,1)S(1)}, f16[2,2,32,4096]{3,2,1,0:T(8,128)(2,1)S(1)}, u32[]{:S(2)}, u32[]{:S(2)}) %collective-permute-start.2) | collective-permute-done | bytes 1048608 | tf_op jit(solution)/shard_map/ppermute | solution.py:21
  169.3 20.3 %collective-permute-done.12 = f16[2,2,32,4096]{3,2,1,0:T(8,128)(2,1)S(1)} collective-permute-done((f16[2,2,32,4096]{3,2,1,0:T(8,128)(2,1)S(1)}, f16[2,2,32,4096]{3,2,1,0:T(8,128)(2,1)S(1)}, u32[]{:S(2)}, u32[]{:S(2)}) %collective-permute-start.12) | collective-permute-done | bytes 1048608 | tf_op jit(solution)/shard_map/ppermute | solution.py:21
  191.8 19.9 %collective-permute-done.17 = f16[2,2,32,4096]{3,2,1,0:T(8,128)(2,1)S(1)} collective-permute-done((f16[2,2,32,4096]{3,2,1,0:T(8,128)(2,1)S(1)}, f16[2,2,32,4096]{3,2,1,0:T(8,128)(2,1)S(1)}, u32[]{:S(2)}, u32[]{:S(2)}) %collective-permute-start.17) | collective-permute-done | bytes 1048608 | tf_op jit(solution)/shard_map/ppermute | solution.py:21
  220.1 16.5 %collective-permute-done.18 = f16[2,32,4096]{2,1,0:T(8,128)(2,1)S(1)} collective-permute-done((f16[2,32,4096]{2,1,0:T(8,128)(2,1)S(1)}, f16[2,32,4096]{2,1,0:T(8,128)(2,1)S(1)}, u32[]{:S(2)}, u32[]{:S(2)}) %collective-permute-start.18) | collective-permute-done | bytes 524320 | tf_op jit(solution)/shard_map/ppermute | solution.py:21
  237.5 14.8 %collective-permute-done.4 = f16[32,4096]{1,0:T(8,128)(2,1)S(1)} collective-permute-done((f16[32,4096]{1,0:T(8,128)(2,1)S(1)}, f16[32,4096]{1,0:T(8,128)(2,1)S(1)}, u32[]{:S(2)}, u32[]{:S(2)}) %collective-permute-start.4) | collective-permute-done | bytes 262176 | tf_op jit(solution)/shard_map/ppermute | solution.py:21
  252.6 5.4 %collective-permute-done.14 = f16[32,4096]{1,0:T(8,128)(2,1)S(1)} collective-permute-done((f16[32,4096]{1,0:T(8,128)(2,1)S(1)}, f16[32,4096]{1,0:T(8,128)(2,1)S(1)}, u32[]{:S(2)}, u32[]{:S(2)}) %collective-permute-start.14) | collective-permute-done | bytes 262176 | tf_op jit(solution)/shard_map/ppermute | solution.py:21
  257.9 4.1 collective-permute-done.19
  262.9 13.1 %collective-permute-done.32 = bf16[128,1024]{1,0:T(8,128)(2,1)S(1)} collective-permute-done((bf16[128,1024]{1,0:T(8,128)(2,1)S(1)}, bf16[128,1024]{1,0:T(8,128)(2,1)S(1)}, u32[]{:S(2)}, u32[]{:S(2)}) %collective-permute-start.32) | collective-permute-done | bytes 262176 | tf_op jit(solution)/shard_map/ppermute | solution.py:21
  278.0 17.6 %collective-permute-done.33 = bf16[2,128,1024]{2,1,0:T(8,128)(2,1)S(1)} collective-permute-done((bf16[2,128,1024]{2,1,0:T(8,128)(2,1)S(1)}, bf16[2,128,1024]{2,1,0:T(8,128)(2,1)S(1)}, u32[]{:S(2)}, u32[]{:S(2)}) %collective-permute-start.33) | collective-permute-done | bytes 524320 | tf_op jit(solution)/shard_map/ppermute | solution.py:21
  299.4 14.2 %collective-permute-done.24 = bf16[128,1024]{1,0:T(8,128)(2,1)S(1)} collective-permute-done((bf16[128,1024]{1,0:T(8,128)(2,1)S(1)}, bf16[128,1024]{1,0:T(8,128)(2,1)S(1)}, u32[]{:S(2)}, u32[]{:S(2)}) %collective-permute-start.24) | collective-permute-done | bytes 262176 | tf_op jit(solution)/shard_map/ppermute | solution.py:21
  317.9 4.0 collective-permute-done.34
  322.2 10.5 %collective-permute-done.25 = bf16[2,128,1024]{2,1,0:T(8,128)(2,1)S(1)} collective-permute-done((bf16[2,128,1024]{2,1,0:T(8,128)(2,1)S(1)}, bf16[2,128,1024]{2,1,0:T(8,128)(2,1)S(1)}, u32[]{:S(2)}, u32[]{:S(2)}) %collective-permute-start.25) | collective-permute-done | bytes 524320 | tf_op jit(solution)/shard_map/ppermute | solution.py:21
  335.0 9.4 %collective-permute-done.30 = bf16[2,2,128,1024]{3,2,1,0:T(8,128)(2,1)S(1)} collective-permute-done((bf16[2,2,128,1024]{3,2,1,0:T(8,128)(2,1)S(1)}, bf16[2,2,128,1024]{3,2,1,0:T(8,128)(2,1)S(1)}, u32[]{:S(2)}, u32[]{:S(2)}) %collective-permute-start.30) | collective-permute-done | bytes 1048608 | tf_op jit(solution)/shard_map/ppermute | solution.py:21
  347.0 19.9 %collective-permute-done.26 = bf16[2,2,128,1024]{3,2,1,0:T(8,128)(2,1)S(1)} collective-permute-done((bf16[2,2,128,1024]{3,2,1,0:T(8,128)(2,1)S(1)}, bf16[2,2,128,1024]{3,2,1,0:T(8,128)(2,1)S(1)}, u32[]{:S(2)}, u32[]{:S(2)}) %collective-permute-start.26) | collective-permute-done | bytes 1048608 | tf_op jit(solution)/shard_map/ppermute | solution.py:21
  368.4 19.1 %collective-permute-done.22 = bf16[2,2,128,1024]{3,2,1,0:T(8,128)(2,1)S(1)} collective-permute-done((bf16[2,2,128,1024]{3,2,1,0:T(8,128)(2,1)S(1)}, bf16[2,2,128,1024]{3,2,1,0:T(8,128)(2,1)S(1)}, u32[]{:S(2)}, u32[]{:S(2)}) %collective-permute-start.22) | collective-permute-done | bytes 1048608 | tf_op jit(solution)/shard_map/ppermute | solution.py:21
  390.3 13.6 %shard_map.81.refs_6_ = f32[1792,4096]{1,0:T(8,128)} custom-call(bf16[2,8,32,1792]{3,2,1,0:T(8,128)(2,1)} %get-tuple-element.22.refs_0_, bf16[2,8,32,1792]{3,2,1,0:T(8,128)(2,1)} %get-tuple-element.23.refs_1_, bf16[2,8,32,1792]{3,2,1,0:T(8,128)(2,1)} %get-tuple-element.24.refs_2_, bf16[2,8,32,1792]{3,2,1,0:T(8,128)(2,1)} %get-tuple-element.25.refs_3_, ...), custom_call_target="tpu_custom_call" | custom-call | flops 7516192768 | bytes 18874368 | tf_op jit(solution)/shard_map/pallas_call | solution.py:102
  403.9 13.7 %shard_map.82.refs_6_ = f32[1792,4096]{1,0:T(8,128)} custom-call(bf16[2,8,32,1792]{3,2,1,0:T(8,128)(2,1)} %get-tuple-element.22.refs_0_, bf16[2,8,32,1792]{3,2,1,0:T(8,128)(2,1)} %get-tuple-element.23.refs_1_, bf16[2,8,32,1792]{3,2,1,0:T(8,128)(2,1)} %get-tuple-element.24.refs_2_, ...), custom_call_target="tpu_custom_call", output_to_operand_aliasing={{}: (6, {})} | custom-call | flops 7516192768 | bytes 18874368 | tf_op jit(solution)/shard_map/pallas_call | solution.py:102
  417.6 13.7 %shard_map.83.refs_6_ = f32[1792,4096]{1,0:T(8,128)} custom-call(bf16[2,8,32,1792]{3,2,1,0:T(8,128)(2,1)} %get-tuple-element.22.refs_0_, bf16[2,8,32,1792]{3,2,1,0:T(8,128)(2,1)} %get-tuple-element.23.refs_1_, bf16[2,8,32,1792]{3,2,1,0:T(8,128)(2,1)} %get-tuple-element.24.refs_2_, ...), custom_call_target="tpu_custom_call", output_to_operand_aliasing={{}: (6, {})} | custom-call | flops 7516192768 | bytes 18874368 | tf_op jit(solution)/shard_map/pallas_call | solution.py:102
  431.3 13.9 %shard_map.84 = f32[1792,4096]{1,0:T(8,128)} custom-call(bf16[2,8,32,1792]{3,2,1,0:T(8,128)(2,1)} %get-tuple-element.22.refs_0_, bf16[2,8,32,1792]{3,2,1,0:T(8,128)(2,1)} %get-tuple-element.23.refs_1_, bf16[2,8,32,1792]{3,2,1,0:T(8,128)(2,1)} %get-tuple-element.24.refs_2_, ...), custom_call_target="tpu_custom_call", output_to_operand_aliasing={{}: (6, {})} | custom-call | flops 7516192768 | bytes 18874368 | tf_op jit(solution)/shard_map/pallas_call | solution.py:102
  (129 shorter events, 55.4 us)
Async XLA Ops:
  3.9 24.3 %collective-permute-start.5 = (bf16[4,2,32,1792]{3,2,1,0:T(8,128)(2,1)S(1)}, bf16[4,2,32,1792]{3,2,1,0:T(8,128)(2,1)}, u32[]{:S(2)}, u32[]{:S(2)}) collective-permute-start(bf16[4,2,32,1792]{3,2,1,0:T(8,128)(2,1)S(1)} %get-tuple-element.37.refs_0_), channel_id=1, source_target_pairs={{0,1},{1,0},{2,3},{3,2},{4,5},{5,4},{6,7},{7,6},{8,9},{9,8},{10,11... | collective-permute-start | bytes 2752520 | tf_op jit(solution)/shard_map/ppermute | solution.py:21
  6.9 41.6 %collective-permute-start = (bf16[4,2,32,1792]{3,2,1,0:T(8,128)(2,1)}, bf16[4,2,32,1792]{3,2,1,0:T(8,128)(2,1)}, u32[]{:S(2)}, u32[]{:S(2)}) collective-permute-start(bf16[4,2,32,1792]{3,2,1,0:T(8,128)(2,1)} %get-tuple-element.34.refs_0_), channel_id=1, source_target_pairs={{0,1},{1,0},{2,3},{3,2},{4,5},{5,4},{6,7},{7,6},{8,9},{9,8},{10,11... | collective-permute-start | bytes 2752520 | tf_op jit(solution)/shard_map/ppermute | solution.py:21
  41.7 72.6 %collective-permute-start.6 = (f32[256,4096]{1,0:T(8,128)}, f32[256,4096]{1,0:T(8,128)}, u32[]{:S(2)}, u32[]{:S(2)}) collective-permute-start(f32[256,4096]{1,0:T(8,128)} %get-tuple-element.17), channel_id=1, source_target_pairs={{0,2},{2,0},{4,6},{6,4},{8,10},{10,8},{12,14},{14,12},{16,18},{18,... | collective-permute-start | bytes 12582920 | tf_op jit(solution)/shard_map/ppermute | solution.py:21
  42.7 71.3 %all-to-all-start = ((bf16[64,2,4096]{2,0,1:T(8,128)(2,1)}), bf16[64,2,4096]{2,0,1:T(8,128)(2,1)S(1)}, u32[]{:S(2)}, u32[]{:S(2)}) async-start(bf16[64,2,4096]{2,0,1:T(8,128)(2,1)} %bitcast.131), calls=%async_computation | async-start | bytes 2097152 | tf_op jit(solution)/shard_map/all_to_all | solution.py:157
  46.3 34.8 %collective-permute-start.10 = (bf16[4,2,32,1792]{3,2,1,0:T(8,128)(2,1)S(1)}, bf16[4,2,32,1792]{3,2,1,0:T(8,128)(2,1)}, u32[]{:S(2)}, u32[]{:S(2)}) collective-permute-start(bf16[4,2,32,1792]{3,2,1,0:T(8,128)(2,1)S(1)} %get-tuple-element.36.refs_0_), channel_id=1, source_target_pairs={{0,1},{1,0},{2,3},{3,2},{4,5},{5,4},{6,7},{7,6},{8,9},{9,8},{10,11... | collective-permute-start | bytes 2752520 | tf_op jit(solution)/shard_map/ppermute | solution.py:21
  48.5 52.1 %collective-permute-start.15 = (bf16[4,2,32,1792]{3,2,1,0:T(8,128)(2,1)S(1)}, bf16[4,2,32,1792]{3,2,1,0:T(8,128)(2,1)}, u32[]{:S(2)}, u32[]{:S(2)}) collective-permute-start(bf16[4,2,32,1792]{3,2,1,0:T(8,128)(2,1)S(1)} %get-tuple-element.35.refs_0_), channel_id=1, source_target_pairs={{0,1},{1,0},{2,3},{3,2},{4,5},{5,4},{6,7},{7,6},{8,9},{9,8},{10,11... | collective-permute-start | bytes 2752520 | tf_op jit(solution)/shard_map/ppermute | solution.py:21
  62.0 58.4 %collective-permute-start.1 = (f32[256,4096]{1,0:T(8,128)}, f32[256,4096]{1,0:T(8,128)}, u32[]{:S(2)}, u32[]{:S(2)}) collective-permute-start(f32[256,4096]{1,0:T(8,128)} %get-tuple-element.15), channel_id=1, source_target_pairs={{0,2},{2,0},{4,6},{6,4},{8,10},{10,8},{12,14},{14,12},{16,18},{18,... | collective-permute-start | bytes 12582920 | tf_op jit(solution)/shard_map/ppermute | solution.py:21
  94.5 30.9 %collective-permute-start.11 = (f32[256,4096]{1,0:T(8,128)}, f32[256,4096]{1,0:T(8,128)}, u32[]{:S(2)}, u32[]{:S(2)}) collective-permute-start(f32[256,4096]{1,0:T(8,128)} %get-tuple-element.19), channel_id=1, source_target_pairs={{0,2},{2,0},{4,6},{6,4},{8,10},{10,8},{12,14},{14,12},{16,18},{18,... | collective-permute-start | bytes 12582920 | tf_op jit(solution)/shard_map/ppermute | solution.py:21
  118.6 26.0 %collective-permute-start.7 = (f16[2,2,32,4096]{3,2,1,0:T(8,128)(2,1)S(1)}, f16[2,2,32,4096]{3,2,1,0:T(8,128)(2,1)S(1)}, u32[]{:S(2)}, u32[]{:S(2)}) collective-permute-start(f16[2,2,32,4096]{3,2,1,0:T(8,128)(2,1)S(1)} %bitcast.143), channel_id=1, source_target_pairs={{0,4},{2,6},{4,0},{6,2},{8,12},{10,14},{12,8},{14,10},{16,20},{18,... | collective-permute-start | bytes 3145736 | tf_op jit(solution)/shard_map/ppermute | solution.py:21
  123.6 43.5 %collective-permute-start.2 = (f16[2,2,32,4096]{3,2,1,0:T(8,128)(2,1)S(1)}, f16[2,2,32,4096]{3,2,1,0:T(8,128)(2,1)S(1)}, u32[]{:S(2)}, u32[]{:S(2)}) collective-permute-start(f16[2,2,32,4096]{3,2,1,0:T(8,128)(2,1)S(1)} %bitcast.144), channel_id=1, source_target_pairs={{0,4},{2,6},{4,0},{6,2},{8,12},{10,14},{12,8},{14,10},{16,20},{18,... | collective-permute-start | bytes 3145736 | tf_op jit(solution)/shard_map/ppermute | solution.py:21
  128.5 61.0 %collective-permute-start.12 = (f16[2,2,32,4096]{3,2,1,0:T(8,128)(2,1)S(1)}, f16[2,2,32,4096]{3,2,1,0:T(8,128)(2,1)S(1)}, u32[]{:S(2)}, u32[]{:S(2)}) collective-permute-start(f16[2,2,32,4096]{3,2,1,0:T(8,128)(2,1)S(1)} %bitcast.145), channel_id=1, source_target_pairs={{0,4},{2,6},{4,0},{6,2},{8,12},{10,14},{12,8},{14,10},{16,20},{18,... | collective-permute-start | bytes 3145736 | tf_op jit(solution)/shard_map/ppermute | solution.py:21
  133.4 78.3 %collective-permute-start.17 = (f16[2,2,32,4096]{3,2,1,0:T(8,128)(2,1)S(1)}, f16[2,2,32,4096]{3,2,1,0:T(8,128)(2,1)S(1)}, u32[]{:S(2)}, u32[]{:S(2)}) collective-permute-start(f16[2,2,32,4096]{3,2,1,0:T(8,128)(2,1)S(1)} %bitcast.146), channel_id=1, source_target_pairs={{0,4},{2,6},{4,0},{6,2},{8,12},{10,14},{12,8},{14,10},{16,20},{18,... | collective-permute-start | bytes 3145736 | tf_op jit(solution)/shard_map/ppermute | solution.py:21
  144.9 69.0 %collective-permute-start.8 = (f16[2,32,4096]{2,1,0:T(8,128)(2,1)S(1)}, f16[2,32,4096]{2,1,0:T(8,128)(2,1)S(1)}, u32[]{:S(2)}, u32[]{:S(2)}) collective-permute-start(f16[2,32,4096]{2,1,0:T(8,128)(2,1)S(1)} %fusion.5), channel_id=1, source_target_pairs={{0,8},{2,10},{4,12},{6,14},{8,0},{10,2},{12,4},{14,6},{16,24},{18,... | collective-permute-start | bytes 1572872 | tf_op jit(solution)/shard_map/ppermute | solution.py:21
  167.4 49.3 %collective-permute-start.3 = (f16[2,32,4096]{2,1,0:T(8,128)(2,1)S(1)}, f16[2,32,4096]{2,1,0:T(8,128)(2,1)S(1)}, u32[]{:S(2)}, u32[]{:S(2)}) collective-permute-start(f16[2,32,4096]{2,1,0:T(8,128)(2,1)S(1)} %fusion.4), channel_id=1, source_target_pairs={{0,8},{2,10},{4,12},{6,14},{8,0},{10,2},{12,4},{14,6},{16,24},{18,... | collective-permute-start | bytes 1572872 | tf_op jit(solution)/shard_map/ppermute | solution.py:21
  189.8 27.4 %collective-permute-start.13 = (f16[2,32,4096]{2,1,0:T(8,128)(2,1)S(1)}, f16[2,32,4096]{2,1,0:T(8,128)(2,1)S(1)}, u32[]{:S(2)}, u32[]{:S(2)}) collective-permute-start(f16[2,32,4096]{2,1,0:T(8,128)(2,1)S(1)} %fusion.6), channel_id=1, source_target_pairs={{0,8},{2,10},{4,12},{6,14},{8,0},{10,2},{12,4},{14,6},{16,24},{18,... | collective-permute-start | bytes 1572872 | tf_op jit(solution)/shard_map/ppermute | solution.py:21
  212.0 24.6 %collective-permute-start.18 = (f16[2,32,4096]{2,1,0:T(8,128)(2,1)S(1)}, f16[2,32,4096]{2,1,0:T(8,128)(2,1)S(1)}, u32[]{:S(2)}, u32[]{:S(2)}) collective-permute-start(f16[2,32,4096]{2,1,0:T(8,128)(2,1)S(1)} %fusion.7), channel_id=1, source_target_pairs={{0,8},{2,10},{4,12},{6,14},{8,0},{10,2},{12,4},{14,6},{16,24},{18,... | collective-permute-start | bytes 1572872 | tf_op jit(solution)/shard_map/ppermute | solution.py:21
  214.0 23.5 %collective-permute-start.9 = (f16[32,4096]{1,0:T(8,128)(2,1)S(1)}, f16[32,4096]{1,0:T(8,128)(2,1)S(1)}, u32[]{:S(2)}, u32[]{:S(2)}) collective-permute-start(f16[32,4096]{1,0:T(8,128)(2,1)S(1)} %fusion.25), channel_id=1, source_target_pairs={{0,16},{2,18},{4,20},{6,22},{8,24},{10,26},{12,28},{14,30},{16,0},... | collective-permute-start | bytes 786440 | tf_op jit(solution)/shard_map/ppermute | solution.py:21
  216.8 35.5 %collective-permute-start.4 = (f16[32,4096]{1,0:T(8,128)(2,1)S(1)}, f16[32,4096]{1,0:T(8,128)(2,1)S(1)}, u32[]{:S(2)}, u32[]{:S(2)}) collective-permute-start(f16[32,4096]{1,0:T(8,128)(2,1)S(1)} %fusion.24), channel_id=1, source_target_pairs={{0,16},{2,18},{4,20},{6,22},{8,24},{10,26},{12,28},{14,30},{16,0},... | collective-permute-start | bytes 786440 | tf_op jit(solution)/shard_map/ppermute | solution.py:21
  217.4 40.5 %collective-permute-start.14 = (f16[32,4096]{1,0:T(8,128)(2,1)S(1)}, f16[32,4096]{1,0:T(8,128)(2,1)S(1)}, u32[]{:S(2)}, u32[]{:S(2)}) collective-permute-start(f16[32,4096]{1,0:T(8,128)(2,1)S(1)} %fusion.26), channel_id=1, source_target_pairs={{0,16},{2,18},{4,20},{6,22},{8,24},{10,26},{12,28},{14,30},{16,0},... | collective-permute-start | bytes 786440 | tf_op jit(solution)/shard_map/ppermute | solution.py:21
  236.7 25.3 %collective-permute-start.19 = (f16[32,4096]{1,0:T(8,128)(2,1)S(1)}, f16[32,4096]{1,0:T(8,128)(2,1)S(1)}, u32[]{:S(2)}, u32[]{:S(2)}) collective-permute-start(f16[32,4096]{1,0:T(8,128)(2,1)S(1)} %fusion.27), channel_id=1, source_target_pairs={{0,16},{2,18},{4,20},{6,22},{8,24},{10,26},{12,28},{14,30},{16,0},... | collective-permute-start | bytes 786440 | tf_op jit(solution)/shard_map/ppermute | solution.py:21
  276.1 19.5 %collective-permute-start.33 = (bf16[2,128,1024]{2,1,0:T(8,128)(2,1)S(1)}, bf16[2,128,1024]{2,1,0:T(8,128)(2,1)S(1)}, u32[]{:S(2)}, u32[]{:S(2)}) collective-permute-start(bf16[2,128,1024]{2,1,0:T(8,128)(2,1)S(1)} %get-tuple-element.63), channel_id=1, source_target_pairs={{0,8},{2,10},{4,12},{6,14},{8,0},{10,2},{12,4},{14,6},{16,24},{18,... | collective-permute-start | bytes 1572872 | tf_op jit(solution)/shard_map/ppermute | solution.py:21
  276.1 21.2 %collective-permute-start.28 = (bf16[128,1024]{1,0:T(8,128)(2,1)S(1)}, bf16[128,1024]{1,0:T(8,128)(2,1)S(1)}, u32[]{:S(2)}, u32[]{:S(2)}) collective-permute-start(bf16[128,1024]{1,0:T(8,128)(2,1)S(1)} %get-tuple-element.52), channel_id=1, source_target_pairs={{0,16},{2,18},{4,20},{6,22},{8,24},{10,26},{12,28},{14,30},{16,0},... | collective-permute-start | bytes 786440 | tf_op jit(solution)/shard_map/ppermute | solution.py:21
  295.7 26.2 %collective-permute-start.34 = (bf16[2,2,128,1024]{3,2,1,0:T(8,128)(2,1)S(1)}, bf16[2,2,128,1024]{3,2,1,0:T(8,128)(2,1)S(1)}, u32[]{:S(2)}, u32[]{:S(2)}) collective-permute-start(bf16[2,2,128,1024]{3,2,1,0:T(8,128)(2,1)S(1)} %get-tuple-element.46), channel_id=1, source_target_pairs={{0,4},{2,6},{4,0},{6,2},{8,12},{10,14},{12,8},{14,10},{16,20},{18,... | collective-permute-start | bytes 3145736 | tf_op jit(solution)/shard_map/ppermute | solution.py:21
  297.4 18.9 %collective-permute-start.29 = (bf16[2,128,1024]{2,1,0:T(8,128)(2,1)S(1)}, bf16[2,128,1024]{2,1,0:T(8,128)(2,1)S(1)}, u32[]{:S(2)}, u32[]{:S(2)}) collective-permute-start(bf16[2,128,1024]{2,1,0:T(8,128)(2,1)S(1)} %get-tuple-element.65), channel_id=1, source_target_pairs={{0,8},{2,10},{4,12},{6,14},{8,0},{10,2},{12,4},{14,6},{16,24},{18,... | collective-permute-start | bytes 1572872 | tf_op jit(solution)/shard_map/ppermute | solution.py:21
  313.7 19.0 %collective-permute-start.25 = (bf16[2,128,1024]{2,1,0:T(8,128)(2,1)S(1)}, bf16[2,128,1024]{2,1,0:T(8,128)(2,1)S(1)}, u32[]{:S(2)}, u32[]{:S(2)}) collective-permute-start(bf16[2,128,1024]{2,1,0:T(8,128)(2,1)S(1)} %get-tuple-element.67), channel_id=1, source_target_pairs={{0,8},{2,10},{4,12},{6,14},{8,0},{10,2},{12,4},{14,6},{16,24},{18,... | collective-permute-start | bytes 1572872 | tf_op jit(solution)/shard_map/ppermute | solution.py:21
  316.5 27.9 %collective-permute-start.30 = (bf16[2,2,128,1024]{3,2,1,0:T(8,128)(2,1)S(1)}, bf16[2,2,128,1024]{3,2,1,0:T(8,128)(2,1)S(1)}, u32[]{:S(2)}, u32[]{:S(2)}) collective-permute-start(bf16[2,2,128,1024]{3,2,1,0:T(8,128)(2,1)S(1)} %get-tuple-element.56), channel_id=1, source_target_pairs={{0,4},{2,6},{4,0},{6,2},{8,12},{10,14},{12,8},{14,10},{16,20},{18,... | collective-permute-start | bytes 3145736 | tf_op jit(solution)/shard_map/ppermute | solution.py:21
  322.1 66.9 %collective-permute-start.35 = (bf16[8,128,1024]{2,1,0:T(8,128)(2,1)S(1)}, bf16[8,128,1024]{2,1,0:T(8,128)(2,1)S(1)}, u32[]{:S(2)}, u32[]{:S(2)}) collective-permute-start(bf16[8,128,1024]{2,1,0:T(8,128)(2,1)S(1)} %bitcast.132), channel_id=1, source_target_pairs={{0,2},{2,0},{4,6},{6,4},{8,10},{10,8},{12,14},{14,12},{16,18},{18,... | collective-permute-start | bytes 6291464 | tf_op jit(solution)/shard_map/ppermute | solution.py:21
  332.8 34.0 %collective-permute-start.26 = (bf16[2,2,128,1024]{3,2,1,0:T(8,128)(2,1)S(1)}, bf16[2,2,128,1024]{3,2,1,0:T(8,128)(2,1)S(1)}, u32[]{:S(2)}, u32[]{:S(2)}) collective-permute-start(bf16[2,2,128,1024]{3,2,1,0:T(8,128)(2,1)S(1)} %get-tuple-element.58), channel_id=1, source_target_pairs={{0,4},{2,6},{4,0},{6,2},{8,12},{10,14},{12,8},{14,10},{16,20},{18,... | collective-permute-start | bytes 3145736 | tf_op jit(solution)/shard_map/ppermute | solution.py:21
  344.6 59.4 %collective-permute-start.31 = (bf16[8,128,1024]{2,1,0:T(8,128)(2,1)S(1)}, bf16[8,128,1024]{2,1,0:T(8,128)(2,1)}, u32[]{:S(2)}, u32[]{:S(2)}) collective-permute-start(bf16[8,128,1024]{2,1,0:T(8,128)(2,1)S(1)} %bitcast.134), channel_id=1, source_target_pairs={{0,2},{2,0},{4,6},{6,4},{8,10},{10,8},{12,14},{14,12},{16,18},{18,... | collective-permute-start | bytes 6291464 | tf_op jit(solution)/shard_map/ppermute | solution.py:21
  345.8 41.7 %collective-permute-start.22 = (bf16[2,2,128,1024]{3,2,1,0:T(8,128)(2,1)S(1)}, bf16[2,2,128,1024]{3,2,1,0:T(8,128)(2,1)S(1)}, u32[]{:S(2)}, u32[]{:S(2)}) collective-permute-start(bf16[2,2,128,1024]{3,2,1,0:T(8,128)(2,1)S(1)} %get-tuple-element.60), channel_id=1, source_target_pairs={{0,4},{2,6},{4,0},{6,2},{8,12},{10,14},{12,8},{14,10},{16,20},{18,... | collective-permute-start | bytes 3145736 | tf_op jit(solution)/shard_map/ppermute | solution.py:21
  367.1 50.5 %collective-permute-start.27 = (bf16[8,128,1024]{2,1,0:T(8,128)(2,1)S(1)}, bf16[8,128,1024]{2,1,0:T(8,128)(2,1)}, u32[]{:S(2)}, u32[]{:S(2)}) collective-permute-start(bf16[8,128,1024]{2,1,0:T(8,128)(2,1)S(1)} %bitcast.140), channel_id=1, source_target_pairs={{0,2},{2,0},{4,6},{6,4},{8,10},{10,8},{12,14},{14,12},{16,18},{18,... | collective-permute-start | bytes 6291464 | tf_op jit(solution)/shard_map/ppermute | solution.py:21
  389.0 42.3 %collective-permute-start.23 = (bf16[8,128,1024]{2,1,0:T(8,128)(2,1)}, bf16[8,128,1024]{2,1,0:T(8,128)(2,1)}, u32[]{:S(2)}, u32[]{:S(2)}) collective-permute-start(bf16[8,128,1024]{2,1,0:T(8,128)(2,1)} %bitcast.36.refs_4_), channel_id=1, source_target_pairs={{0,2},{2,0},{4,6},{6,4},{8,10},{10,8},{12,14},{14,12},{16,18},{18,... | collective-permute-start | bytes 6291464 | tf_op jit(solution)/shard_map/ppermute | solution.py:21
  (19 other events, 363.8 us)

commit v2 on v0

v2 whole, which is shorter than its diff:
```python
import math

import jax
import jax.numpy as jnp
from jax import lax
from jax.experimental import pallas as pl
from jax.experimental.pallas import tpu as pltpu
from jax.sharding import PartitionSpec as P

SEQ_LEN = 256
RETAIN_WEIGHT = 2.0
F32, BF16, WIRE = jnp.float32, jnp.bfloat16, jnp.float16
VMEM_LIMIT = 56 * 1024 * 1024


def bits_of(count):
    return count.bit_length() - 1


def flip(array, axis, mask):
    return lax.ppermute(array, axis, [(i, i ^ mask) for i in range(lax.axis_size(axis))])


def slot_of(chip, nb):
    slot = 0
    for b in range(nb):
        slot = slot * 2 + ((chip >> b) & 1)
    return slot


def project(place, groups, rows, at, w_down, start, width, held, before):
    arrays = [g for g, _ in groups]
    units = w_down.shape[0]
    chips, tok_rows = (held.shape[1:3]) if held is not None else (arrays[0].shape[0] * len(arrays), arrays[0].shape[2])
    nb = bits_of(chips)
    block = min(1024, width)
    first = start // block

    def kernel(place_ref, *refs):
        group_refs, w_ref = refs[: len(arrays)], refs[len(arrays)]
        if arrays:
            theirs_ref, mine_ref, rows_ref = refs[-3:]

            @pl.when(pl.program_id(0) == 0)
            def _():
                for d, (ref, (_, from_row)) in enumerate(zip(group_refs, groups)):
                    per = ref.shape[0]
                    for t in range(per):
                        slot = slot_of(place_ref[1] ^ ((place_ref[2] ^ d) * per + t), nb)
                        for parity in range(2):
                            rows_ref[place_ref[0] ^ parity, slot] = ref[t, parity, from_row : from_row + rows]

        else:
            (theirs_ref, mine_ref), rows_ref = refs[-2:], refs[1]
        for parity, out_ref in ((1, theirs_ref), (0, mine_ref)):
            lhs = rows_ref[parity].reshape(chips * rows, units)
            out_ref[...] = jnp.dot(lhs, w_ref[...], preferred_element_type=F32)

    chunk = pl.BlockSpec((2, chips, rows, units), lambda i, _: (0, 0, at // rows, 0))
    column = pl.BlockSpec((chips * rows, block), lambda i, _: (0, i))
    partial = jax.ShapeDtypeStruct((chips * rows, width), F32)
    out_specs, out_shape, alias = [column, column], [partial, partial], {}
    args = [*arrays, w_down]
    in_specs = [pl.BlockSpec(g.shape, lambda i, _: (0, 0, 0, 0)) for g in arrays]
    in_specs.append(pl.BlockSpec((units, block), lambda i, _: (0, first + i)))
    if arrays:
        out_specs.append(chunk)
        out_shape.append(jax.ShapeDtypeStruct((2, chips, tok_rows, units), BF16))
    if held is not None:
        if arrays:
            alias = {len(args) + 1: 2}
        args.append(held)
        in_specs.append(pl.BlockSpec(memory_space=pl.ANY) if arrays else chunk)
    args += before
    in_specs += [pl.BlockSpec(memory_space=pl.ANY)] * len(before)
    return pl.pallas_call(
        kernel,
        grid_spec=pltpu.PrefetchScalarGridSpec(
            num_scalar_prefetch=1, grid=(width // block,), in_specs=in_specs, out_specs=out_specs
        ),
        out_shape=out_shape,
        input_output_aliases=alias,
        compiler_params=pltpu.CompilerParams(vmem_limit_bytes=VMEM_LIMIT),
        cost_estimate=pl.CostEstimate(
            flops=4 * chips * rows * units * width,
            bytes_accessed=2 * units * width + 8 * chips * rows * (width + units),
            transcendentals=0,
        ),
    )(place, *args)


def gradient(place, rows, firsts, slopes):
    _, chips, tok_rows, units = rows.shape
    counts, feats = [f.shape[1] for f in firsts], firsts[0].shape[2]
    count = sum(counts)
    width = slopes[0][0].shape[2]
    nb = bits_of(chips)
    block = min(512, width)
    each = width // block

    def kernel(place_ref, rows_ref, *refs):
        first_refs, refs = refs[: len(firsts)], refs[len(firsts) :]
        out_ref, all_ref = refs[-2:]
        for parity in range(2):
            for owner in range(chips):
                slot, row = slot_of(place_ref[1] ^ owner, nb), 0
                for n, first_ref in zip(counts, first_refs):
                    all_ref[parity, slot, row : row + n] = first_ref[2 * owner + (place_ref[0] ^ parity)]
                    row += n
        for q in range(len(slopes)):

            @pl.when(pl.program_id(0) // each == q)
            def _():
                for parity in range(2):
                    all_ref[parity, :, count:] = refs[2 * q + parity][...]

        total = None
        for parity in range(2):
            term = lax.dot_general(
                rows_ref[parity].reshape(chips * tok_rows, units),
                all_ref[parity].reshape(chips * tok_rows, block),
                (((0,), (0,)), ((), ())),
                preferred_element_type=F32,
            )
            total = term if total is None else total + term
        out_ref[...] = total

    in_specs = [
        pl.BlockSpec(rows.shape, lambda i, _: (0, 0, 0, 0), pipeline_mode=pl.Buffered(1)),
        *[pl.BlockSpec((2 * chips, n, block), lambda i, _: (0, 0, i)) for n in counts],
    ]
    for q in range(len(slopes)):
        in_specs += [
            pl.BlockSpec(
                (chips, tok_rows - count, block), lambda i, _, q=q: (0, 0, jnp.clip(i - q * each, 0, each - 1))
            )
        ] * 2
    return pl.pallas_call(
        kernel,
        grid_spec=pltpu.PrefetchScalarGridSpec(
            num_scalar_prefetch=1,
            grid=(feats // block,),
            in_specs=in_specs,
            out_specs=pl.BlockSpec((units, block), lambda i, _: (0, i)),
            scratch_shapes=[pltpu.VMEM((2, chips, tok_rows, block), BF16)],
        ),
        out_shape=jax.ShapeDtypeStruct((units, feats), F32),
        compiler_params=pltpu.CompilerParams(vmem_limit_bytes=VMEM_LIMIT),
        cost_estimate=pl.CostEstimate(
            flops=4 * chips * tok_rows * units * feats,
            bytes_accessed=4 * chips * tok_rows * (units + feats) + 4 * units * feats,
            transcendentals=0,
        ),
    )(place, rows, *firsts, *[s for pair in slopes for s in pair])


def cut(total, left, b):
    at = left.index(b)
    sent = lax.index_in_dim(total, 1, at, keepdims=False).astype(WIRE)
    return lax.index_in_dim(total, 0, at, keepdims=False), flip(sent, "dp", 2 << b)


def nothing(array):
    return array[(0,) * array.ndim] * 0


def gather_chips(block, order):
    have = []
    for b in order:
        have = sorted([*have, b])
        block = jnp.stack([block, flip(block, "dp", 2 << b)], axis=have.index(b))
    return block.reshape((2 ** len(order),) + block.shape[len(order) :])


def pass_pair(array):
    pieces = jnp.split(array.astype(WIRE), 4, axis=0)
    return jnp.concatenate([flip(p, "dp", 1) for p in pieces]).astype(F32)


def per_device(resid_in, hidden, w_down, frozen, steer, forget_flags):
    n_dp, n_shard = lax.axis_size("dp"), lax.axis_size("shard")
    chips = n_dp // 2
    nb = bits_of(chips)
    tok_rows, feats = resid_in.shape
    units = hidden.shape[1]
    dp, shard = lax.axis_index("dp"), lax.axis_index("shard")
    core, chip = dp % 2, dp // 2
    place = jnp.stack([core, chip, shard]).astype(jnp.int32)
    up = list(range(nb))
    orders = [up, [*up[1:2], *up[:1], *up[2:]]]
    half = feats // 2
    unit = tok_rows // 8
    spans = [unit * n for n in (3, 3, 2)]
    starts = [sum(spans[:k]) for k in range(len(spans))]
    sends = [(0, spans[0]), (spans[0], tok_rows)]

    def pick(stack, at):
        return lax.dynamic_index_in_dim(stack, at, 0, keepdims=False)

    own = hidden.reshape(chips // n_shard, 2, tok_rows, units)
    far = [
        [flip(lax.slice_in_dim(own, at, end, axis=2), "shard", d) for d in range(1, n_shard)] for at, end in sends
    ]
    found = []
    for d in range(n_shard):
        part = lax.dynamic_slice_in_dim(frozen, (shard ^ d) * feats, feats, axis=1)
        if d:
            part = flip(part + nothing(far[0][0]), "shard", d)
        found.append(part)
    found = jnp.stack(found)
    target_rows = jnp.concatenate([pick(found, shard ^ e) for e in range(n_shard)])
    seq = (dp * tok_rows + jnp.arange(tok_rows, dtype=jnp.int32)) // SEQ_LEN
    match = seq[:, None] == jnp.arange(forget_flags.shape[0], dtype=jnp.int32)[None, :]
    is_forget = jnp.sum(jnp.where(match, forget_flags[None, :], 0), axis=1, keepdims=True) > 0
    scale = jnp.where(is_forget, 1.0, RETAIN_WEIGHT).astype(F32) * (1.0 / math.sqrt(tok_rows * n_dp))
    target = jnp.where(is_forget, steer.astype(F32)[None, :], target_rows.astype(F32))

    held, firsts, updated, sloped, sums = None, [], [], [], {}

    def multiply(k, s, before):
        nonlocal held
        piece = min(k, 1)
        source = [] if s else [(own, starts[k])] + [(f, starts[k] - sends[piece][0]) for f in far[piece]]
        theirs, mine, *out = project(place, source, spans[k], starts[k], w_down, s * half, half, held, before)
        held = out[0] if out else held
        sums[k, s] = mine, pass_pair(theirs), orders[s]
        return nothing(theirs)

    def advance(k, zero):
        kept_all, changed, slopes = [], [], []
        for s in range(len(orders)):
            kept, came, order = sums[k, s]
            total = kept + came.astype(F32) + zero
            if len(order) == nb:
                total = total.reshape((2,) * nb + (spans[k], half))
            if order:
                sums[k, s] = *cut(total, sorted(order), order[0]), order[1:]
                kept_all.append(sums[k, s][0])
                continue
            here, columns = slice(starts[k], starts[k] + spans[k]), slice(s * half, (s + 1) * half)
            residual = resid_in[here, columns].astype(F32) + total
            changed.append(residual.astype(BF16))
            slopes.append((scale[here] * (residual - target[here, columns])).astype(BF16))
            kept_all.append(slopes[-1])
        if changed:
            updated.append(jnp.concatenate(changed, axis=1))
            sloped.append(slopes)
        return kept_all

    for s in range(len(orders)):
        multiply(0, s, [])
    zero = 0.0
    for k in range(len(spans)):
        advance(k, 0.0)
        kept = advance(k, zero)
        if k + 1 == len(spans):
            break
        for s in range(len(orders)):
            kept = advance(k, multiply(k + 1, s, kept))
        while len(sloped) == k:
            kept = advance(k, 0.0)
        firsts.append(lax.all_gather(jnp.concatenate(sloped[k], axis=1), "dp"))
        zero = sum(nothing(b).astype(F32) for b in kept)
    while len(sloped) < len(spans):
        advance(len(spans) - 1, 0.0)

    gathered, streams = [], 4
    width = feats // streams
    for q in range(streams):
        s, at = divmod(q * width, half)
        block = gather_chips(sloped[-1][s][:, at : at + width], orders[q % 2][::-1])
        gathered.append((block, flip(block, "dp", 1)))
    return jnp.concatenate(updated), gradient(place, held, firsts, gathered)


def solution(mesh):
    in_specs = (
        P("dp", "shard"),
        P("shard", "dp"),
        P("dp", "shard"),
        P(("dp", "shard"), None),
        P("shard"),
        P(),
    )
    out_specs = (P("dp", "shard"), P("dp", "shard"))
    return jax.shard_map(
        per_device, mesh=mesh, in_specs=in_specs, out_specs=out_specs, check_vma=False
    )
```

time: 681 us -> 409 us (0.60)
  waiting for transfers between devices: 550 us -> 175 us
  Pallas kernels: 0 us -> 108 us
  matrix products: 77.7 us -> 0 us
  starting transfers between devices: 3.88 us -> 48.6 us
  other arithmetic: 3.67 us -> 29.7 us
  between operations: 13.8 us -> 20.8 us
    reduce_scatter x1 -> x0, waiting for transfers between devices: 313 us -> none  [per_device(): lax.psum_scatter(jnp.dot(whole_hidden, w_down, preferred_element_type=jnp...]
    all_gather x2, waiting for transfers between devices: 223 us -> 0.01 us  [per_device(): firsts.append(lax.all_gather(jnp.concatenate(sloped[k], axis=1), 'dp'))]
    ppermute x0 -> x61, waiting for transfers between devices: none -> 175 us  [flip(): lax.ppermute(array, axis, [(i, i ^ mask) for i in range(lax.axis_size(axi...]
    pallas_call x0 -> x7, Pallas kernels: none -> 108 us  [the longest x6 66.7 us: project(): pl.pallas_call(kernel, grid_spec=pltpu.PrefetchScalarGridSpec(num_scalar_...]
    dot_general x2 -> x0, matrix products: 77.7 us -> none  [the longest x1 39 us: per_device(): lax.dot_general(whole_hidden, all_slopes, (((0,), (0,)), ((), ())), prefe...]
    ppermute x0 -> x61, starting transfers between devices: none -> 48.5 us  [flip(): lax.ppermute(array, axis, [(i, i ^ mask) for i in range(lax.axis_size(axi...]
    unnamed x9 -> x54, local copies, waits for them, and re-layouts: 30.6 us -> 6.51 us
    slice x0 -> x16, local copies, waits for them, and re-layouts: none -> 17.7 us  [the longest x9 11 us: nothing(): return array[(0,) * array.ndim] * 0]
  transfers between devices with their start and end apart: 4 -> 63, of which waited for: 4 -> 27; matrix products, arithmetic and copies ran while one was open for 0% -> 11% of each run, Pallas kernels for 0% -> 16%
where the time goes in v2:
time: 409 us
  waiting for transfers between devices  175 us (43%)
  Pallas kernels  108 us (26%)
  starting transfers between devices  48.6 us (12%)
  other arithmetic  29.7 us (7%)
  local copies, waits for them, and re-layouts  26 us (6%)
  between operations  20.8 us (5%)
    ppermute x61, waiting for transfers between devices, flip(): lax.ppermute(array, axis, [(i, i ^ mask) for i in range(lax.axis_size(axi...  175 us
    pallas_call x6, Pallas kernels, project(): pl.pallas_call(kernel, grid_spec=pltpu.PrefetchScalarGridSpec(num_scalar_...  66.7 us
    ppermute x61, starting transfers between devices, flip(): lax.ppermute(array, axis, [(i, i ^ mask) for i in range(lax.axis_size(axi...  48.5 us
    pallas_call x1, Pallas kernels, gradient(): pl.pallas_call(kernel, grid_spec=pltpu.PrefetchScalarGridSpec(num_scalar_...  41.7 us
    slice x9, local copies, waits for them, and re-layouts, nothing(): return array[(0,) * array.ndim] * 0  11 us
    convert_element_type x6, other arithmetic, pass_pair(): pieces = jnp.split(array.astype(WIRE), 4, axis=0)  8.58 us
  transfers between devices with their start and end apart: 63, of which 27 were waited for; matrix products, arithmetic and copies ran while one was open for 11% of the time, Pallas kernels for 16%

profile of v2, /device:TPU:0, one launch (start us, length us, event | category | flops | bytes accessed | tf_op | source)
XLA Modules:
  0.0 408.7 jit_solution(9192279316321729476)
XLA Ops:
  7.2 2.5 slice.294
  9.7 2.9 collective-permute-start
  12.7 3.2 slice.299
  16.7 27.3 %collective-permute-done.refs_1_ = bf16[4,2,48,1792]{3,2,1,0:T(8,128)(2,1)} collective-permute-done((bf16[4,2,48,1792]{3,2,1,0:T(8,128)(2,1)}, bf16[4,2,48,1792]{3,2,1,0:T(8,128)(2,1)}, u32[]{:S(2)}, u32[]{:S(2)}) %collective-permute-start) | collective-permute-done | bytes 1376288 | tf_op jit(solution)/shard_map/ppermute | solution.py:21
  44.0 12.8 %shard_map.77 = (f32[384,2048]{1,0:T(8,128)}, f32[384,2048]{1,0:T(8,128)}, bf16[2,8,128,1792]{3,2,1,0:T(8,128)(2,1)}) custom-call(s32[3]{0:T(128)} %pad_add_fusion.place_ref, bf16[4,2,128,1792]{3,2,1,0:T(8,128)(2,1)} %bitcast.185, bf16[4,2,48,1792]{3,2,1,0:T(8,128)(2,1)} %collective-permute-done.refs_1_, bf16[1792,4096]{1,0:T(8,128)(2,1)} %refs_0_.5), custom_call_target="tpu_custom_call" | custom-call | flops 5637144576 | bytes 19136512 | tf_op jit(solution)/shard_map/pallas_call | solution.py:76
  60.3 10.8 %shard_map.78 = (f32[384,2048]{1,0:T(8,128)}, f32[384,2048]{1,0:T(8,128)}) custom-call(s32[3]{0:T(128)} %pad_add_fusion.place_ref, bf16[1792,4096]{1,0:T(8,128)(2,1)} %refs_0_.5, bf16[2,8,128,1792]{3,2,1,0:T(8,128)(2,1)} %get-tuple-element.19.refs_1_.refs_3_), custom_call_target="tpu_custom_call" | custom-call | flops 5637144576 | bytes 19136512 | tf_op jit(solution)/shard_map/pallas_call | solution.py:76
  71.0 2.2 convert_element_type.245
  77.9 2.1 collective-permute-start.21
  84.5 19.0 %collective-permute-done.21 = bf16[64,4096]{1,0:T(8,128)(2,1)S(1)} collective-permute-done((bf16[64,4096]{1,0:T(8,128)(2,1)S(1)}, bf16[64,4096]{1,0:T(8,128)(2,1)S(1)}, u32[]{:S(2)}, u32[]{:S(2)}) %collective-permute-start.21) | collective-permute-done | bytes 524320 | tf_op jit(solution)/shard_map/ppermute | solution.py:21
  112.6 13.1 %shard_map.79 = (f32[384,2048]{1,0:T(8,128)}, f32[384,2048]{1,0:T(8,128)}, bf16[2,8,128,1792]{3,2,1,0:T(8,128)(2,1)}) custom-call(s32[3]{0:T(128)} %pad_add_fusion.place_ref, bf16[4,2,128,1792]{3,2,1,0:T(8,128)(2,1)} %bitcast.186, bf16[4,2,80,1792]{3,2,1,0:T(8,128)(2,1)} %copy-done, bf16[1792,4096]{1,0:T(8,128)(2,1)} %refs_0_.5, ...), custom_call_target="tpu_custom_call", output_to_operand_aliasing={{2}: (4, {})} | custom-call | flops 5637144576 | bytes 19136512 | tf_op jit(solution)/shard_map/pallas_call | solution.py:76
  128.5 2.6 collective-permute-start.13
  132.3 11.1 %shard_map.80 = (f32[384,2048]{1,0:T(8,128)}, f32[384,2048]{1,0:T(8,128)}) custom-call(s32[3]{0:T(128)} %pad_add_fusion.place_ref, bf16[1792,4096]{1,0:T(8,128)(2,1)} %refs_0_.5, bf16[2,8,128,1792]{3,2,1,0:T(8,128)(2,1)} %get-tuple-element.23.refs_1_.refs_3_, f32[48,2048]{1,0:T(8,128)} %get-tuple-element.99.refs_2_, f32[48,2048]{1,0:T(8,128)} %get-tuple-element.97.refs_3_), custom_call_target="tpu_custom_call" | custom-call | flops 5637144576 | bytes 19136512 | tf_op jit(solution)/shard_map/pallas_call | solution.py:76
  162.0 17.8 %collective-permute-done.20 = f16[2,2,48,2048]{3,2,1,0:T(8,128)(2,1)S(1)} collective-permute-done((f16[2,2,48,2048]{3,2,1,0:T(8,128)(2,1)S(1)}, f16[2,2,48,2048]{3,2,1,0:T(8,128)(2,1)S(1)}, u32[]{:S(2)}, u32[]{:S(2)}) %collective-permute-start.20) | collective-permute-done | bytes 786464 | tf_op jit(solution)/shard_map/ppermute | solution.py:21
  181.0 14.4 %collective-permute-done.27 = f16[2,2,48,2048]{3,2,1,0:T(8,128)(2,1)S(1)} collective-permute-done((f16[2,2,48,2048]{3,2,1,0:T(8,128)(2,1)S(1)}, f16[2,2,48,2048]{3,2,1,0:T(8,128)(2,1)S(1)}, u32[]{:S(2)}, u32[]{:S(2)}) %collective-permute-start.27) | collective-permute-done | bytes 786464 | tf_op jit(solution)/shard_map/ppermute | solution.py:21
  196.8 10.5 %shard_map.81 = (f32[256,2048]{1,0:T(8,128)}, f32[256,2048]{1,0:T(8,128)}, bf16[2,8,128,1792]{3,2,1,0:T(8,128)(2,1)}) custom-call(s32[3]{0:T(128)} %pad_add_fusion.place_ref, bf16[4,2,128,1792]{3,2,1,0:T(8,128)(2,1)} %bitcast.187, bf16[4,2,80,1792]{3,2,1,0:T(8,128)(2,1)} %copy-done, bf16[1792,4096]{1,0:T(8,128)(2,1)} %refs_0_.5, ...), custom_call_target="tpu_custom_call", output_to_operand_aliasing={{2}: (4, {})} | custom-call | flops 3758096384 | bytes 15204352 | tf_op jit(solution)/shard_map/pallas_call | solution.py:76
  209.2 5.6 %collective-permute-done.22 = f16[2,48,2048]{2,1,0:T(8,128)(2,1)S(1)} collective-permute-done((f16[2,48,2048]{2,1,0:T(8,128)(2,1)S(1)}, f16[2,48,2048]{2,1,0:T(8,128)(2,1)S(1)}, u32[]{:S(2)}, u32[]{:S(2)}) %collective-permute-start.22) | collective-permute-done | bytes 393248 | tf_op jit(solution)/shard_map/ppermute | solution.py:21
  216.8 2.7 collective-permute-start.30
  219.5 8.5 %shard_map.82 = (f32[256,2048]{1,0:T(8,128)}, f32[256,2048]{1,0:T(8,128)}) custom-call(s32[3]{0:T(128)} %pad_add_fusion.place_ref, bf16[1792,4096]{1,0:T(8,128)(2,1)} %refs_0_.5, bf16[2,8,128,1792]{3,2,1,0:T(8,128)(2,1)} %get-tuple-element.28.refs_1_.rows_ref, f32[48,2048]{1,0:T(8,128)} %get-tuple-element.95.refs_2_, f32[48,2048]{1,0:T(8,128)} %get-tuple-element.93.refs_3_), custom_call_target="tpu_custom_call" | custom-call | flops 3758096384 | bytes 15204352 | tf_op jit(solution)/shard_map/pallas_call | solution.py:76
  229.8 8.6 %collective-permute-done.28 = f16[48,2048]{1,0:T(8,128)(2,1)S(1)} collective-permute-done((f16[48,2048]{1,0:T(8,128)(2,1)S(1)}, f16[48,2048]{1,0:T(8,128)(2,1)S(1)}, u32[]{:S(2)}, u32[]{:S(2)}) %collective-permute-start.28) | collective-permute-done | bytes 196640 | tf_op jit(solution)/shard_map/ppermute | solution.py:21
  238.4 4.1 %collective-permute-done.30 = f16[48,2048]{1,0:T(8,128)(2,1)S(1)} collective-permute-done((f16[48,2048]{1,0:T(8,128)(2,1)S(1)}, f16[48,2048]{1,0:T(8,128)(2,1)S(1)}, u32[]{:S(2)}, u32[]{:S(2)}) %collective-permute-start.30) | collective-permute-done | bytes 196640 | tf_op jit(solution)/shard_map/ppermute | solution.py:21
  257.9 11.2 %collective-permute-done.35 = f16[2,2,32,2048]{3,2,1,0:T(8,128)(2,1)S(1)} collective-permute-done((f16[2,2,32,2048]{3,2,1,0:T(8,128)(2,1)S(1)}, f16[2,2,32,2048]{3,2,1,0:T(8,128)(2,1)S(1)}, u32[]{:S(2)}, u32[]{:S(2)}) %collective-permute-start.35) | collective-permute-done | bytes 524320 | tf_op jit(solution)/shard_map/ppermute | solution.py:21
  271.5 12.4 %collective-permute-done.36 = f16[2,32,2048]{2,1,0:T(8,128)(2,1)S(1)} collective-permute-done((f16[2,32,2048]{2,1,0:T(8,128)(2,1)S(1)}, f16[2,32,2048]{2,1,0:T(8,128)(2,1)S(1)}, u32[]{:S(2)}, u32[]{:S(2)}) %collective-permute-start.36) | collective-permute-done | bytes 262176 | tf_op jit(solution)/shard_map/ppermute | solution.py:21
  284.0 29.8 %collective-permute-done.42 = f16[2,2,32,2048]{3,2,1,0:T(8,128)(2,1)S(1)} collective-permute-done((f16[2,2,32,2048]{3,2,1,0:T(8,128)(2,1)S(1)}, f16[2,2,32,2048]{3,2,1,0:T(8,128)(2,1)S(1)}, u32[]{:S(2)}, u32[]{:S(2)}) %collective-permute-start.42) | collective-permute-done | bytes 524320 | tf_op jit(solution)/shard_map/ppermute | solution.py:21
  315.8 4.6 %collective-permute-done.43 = f16[2,32,2048]{2,1,0:T(8,128)(2,1)S(1)} collective-permute-done((f16[2,32,2048]{2,1,0:T(8,128)(2,1)S(1)}, f16[2,32,2048]{2,1,0:T(8,128)(2,1)S(1)}, u32[]{:S(2)}, u32[]{:S(2)}) %collective-permute-start.43) | collective-permute-done | bytes 262176 | tf_op jit(solution)/shard_map/ppermute | solution.py:21
  323.5 5.0 %collective-permute-done.44 = f16[32,2048]{1,0:T(8,128)(2,1)S(1)} collective-permute-done((f16[32,2048]{1,0:T(8,128)(2,1)S(1)}, f16[32,2048]{1,0:T(8,128)(2,1)S(1)}, u32[]{:S(2)}, u32[]{:S(2)}) %collective-permute-start.44) | collective-permute-done | bytes 131104 | tf_op jit(solution)/shard_map/ppermute | solution.py:21
  328.8 2.9 collective-permute-start.53
  331.9 2.8 collective-permute-start.45
  335.0 4.6 %collective-permute-start.54 = (bf16[2,32,1024]{2,1,0:T(8,128)(2,1)S(1)}, bf16[2,32,1024]{2,1,0:T(8,128)(2,1)S(1)}, u32[]{:S(2)}, u32[]{:S(2)}) collective-permute-start(bf16[2,32,1024]{2,1,0:T(8,128)(2,1)S(1)} %get-tuple-element.115), channel_id=1, source_target_pairs={{0,8},{2,10},{4,12},{6,14},{8,0},{10,2},{12,4},{14,6},{16,24},{18,... | collective-permute-start | bytes 393224 | tf_op jit(solution)/shard_map/ppermute | solution.py:21
  339.8 3.1 collective-permute-start.46
  343.1 2.3 collective-permute-done.50
  351.0 2.7 collective-permute-done.51
  360.2 41.7 %shard_map.83 = f32[1792,4096]{1,0:T(8,128)} custom-call(s32[3]{0:T(128)} %pad_add_fusion.place_ref, bf16[2,8,128,1792]{3,2,1,0:T(8,128)(2,1)} %get-tuple-element.28.refs_1_.rows_ref, bf16[16,48,4096]{2,1,0:T(8,128)(2,1)} %bitcast.218, bf16[16,48,4096]{2,1,0:T(8,128)(2,1)} %bitcast.219, bf16[8,32,1024]{2,1,0:T(8,128)(2,1)} %bitcast.202, ...), custom_call_target="tpu_custom_call" | custom-call | flops 30064771072 | bytes 53477376 | tf_op jit(solution)/shard_map/pallas_call | solution.py:138
  (252 shorter events, 83.0 us)
Async XLA Ops:
  7.2 353.1 %all-gather.5.cloned.1.call-start = ((), (), s32[]{:S(2)}) async-start(), calls=%async_computation | async-start | bytes 6684672 | tf_op jit(solution)/shard_map/all_gather | solution.py:262
  9.7 34.3 %collective-permute-start = (bf16[4,2,48,1792]{3,2,1,0:T(8,128)(2,1)}, bf16[4,2,48,1792]{3,2,1,0:T(8,128)(2,1)}, u32[]{:S(2)}, u32[]{:S(2)}) collective-permute-start(bf16[4,2,48,1792]{3,2,1,0:T(8,128)(2,1)} %slice.294), channel_id=1, source_target_pairs={{0,1},{1,0},{2,3},{3,2},{4,5},{5,4},{6,7},{7,6},{8,9},{9,8},{10,11... | collective-permute-start | bytes 4128776 | tf_op jit(solution)/shard_map/ppermute | solution.py:21
  15.8 95.3 %collective-permute-start.7 = (bf16[4,2,80,1792]{3,2,1,0:T(8,128)(2,1)}, bf16[4,2,80,1792]{3,2,1,0:T(8,128)(2,1)S(1)}, u32[]{:S(2)}, u32[]{:S(2)}) collective-permute-start(bf16[4,2,80,1792]{3,2,1,0:T(8,128)(2,1)} %slice.299), channel_id=1, source_target_pairs={{0,1},{1,0},{2,3},{3,2},{4,5},{5,4},{6,7},{7,6},{8,9},{9,8},{10,11... | collective-permute-start | bytes 6881288 | tf_op jit(solution)/shard_map/ppermute | solution.py:21
  59.2 16.6 %collective-permute-start.1 = (f16[96,2048]{1,0:T(8,128)(2,1)S(1)}, f16[96,2048]{1,0:T(8,128)(2,1)S(1)}, u32[]{:S(2)}, u32[]{:S(2)}) collective-permute-start(f16[96,2048]{1,0:T(8,128)(2,1)S(1)} %get-tuple-element.76), channel_id=1, source_target_pairs={{0,2},{2,0},{4,6},{6,4},{8,10},{10,8},{12,14},{14,12},{16,18},{18,... | collective-permute-start | bytes 1179656 | tf_op jit(solution)/shard_map/ppermute | solution.py:21
  59.2 16.7 %collective-permute-start.4 = (f16[96,2048]{1,0:T(8,128)(2,1)S(1)}, f16[96,2048]{1,0:T(8,128)(2,1)S(1)}, u32[]{:S(2)}, u32[]{:S(2)}) collective-permute-start(f16[96,2048]{1,0:T(8,128)(2,1)S(1)} %get-tuple-element.77), channel_id=1, source_target_pairs={{0,2},{2,0},{4,6},{6,4},{8,10},{10,8},{12,14},{14,12},{16,18},{18,... | collective-permute-start | bytes 1179656 | tf_op jit(solution)/shard_map/ppermute | solution.py:21
  59.7 16.6 %collective-permute-start.3 = (f16[96,2048]{1,0:T(8,128)(2,1)S(1)}, f16[96,2048]{1,0:T(8,128)(2,1)S(1)}, u32[]{:S(2)}, u32[]{:S(2)}) collective-permute-start(f16[96,2048]{1,0:T(8,128)(2,1)S(1)} %get-tuple-element.78), channel_id=1, source_target_pairs={{0,2},{2,0},{4,6},{6,4},{8,10},{10,8},{12,14},{14,12},{16,18},{18,... | collective-permute-start | bytes 1179656 | tf_op jit(solution)/shard_map/ppermute | solution.py:21
  59.8 16.6 %collective-permute-start.2 = (f16[96,2048]{1,0:T(8,128)(2,1)S(1)}, f16[96,2048]{1,0:T(8,128)(2,1)S(1)}, u32[]{:S(2)}, u32[]{:S(2)}) collective-permute-start(f16[96,2048]{1,0:T(8,128)(2,1)S(1)} %get-tuple-element.79), channel_id=1, source_target_pairs={{0,2},{2,0},{4,6},{6,4},{8,10},{10,8},{12,14},{14,12},{16,18},{18,... | collective-permute-start | bytes 1179656 | tf_op jit(solution)/shard_map/ppermute | solution.py:21
  77.9 25.5 %collective-permute-start.21 = (bf16[64,4096]{1,0:T(8,128)(2,1)S(1)}, bf16[64,4096]{1,0:T(8,128)(2,1)S(1)}, u32[]{:S(2)}, u32[]{:S(2)}) collective-permute-start(bf16[64,4096]{1,0:T(8,128)(2,1)S(1)} %get-tuple-element.90), channel_id=1, source_target_pairs={{0,1},{1,0},{2,3},{3,2},{4,5},{5,4},{6,7},{7,6},{8,9},{9,8},{10,11... | collective-permute-start | bytes 1572872 | tf_op jit(solution)/shard_map/ppermute | solution.py:21
  80.1 25.3 %collective-permute-start.5 = (f16[2,2,48,2048]{3,2,1,0:T(8,128)(2,1)S(1)}, f16[2,2,48,2048]{3,2,1,0:T(8,128)(2,1)S(1)}, u32[]{:S(2)}, u32[]{:S(2)}) collective-permute-start(f16[2,2,48,2048]{3,2,1,0:T(8,128)(2,1)S(1)} %bitcast.194), channel_id=1, source_target_pairs={{0,4},{2,6},{4,0},{6,2},{8,12},{10,14},{12,8},{14,10},{16,20},{18,... | collective-permute-start | bytes 2359304 | tf_op jit(solution)/shard_map/ppermute | solution.py:21
  82.8 25.6 %collective-permute-start.12 = (f16[2,2,48,2048]{3,2,1,0:T(8,128)(2,1)S(1)}, f16[2,2,48,2048]{3,2,1,0:T(8,128)(2,1)S(1)}, u32[]{:S(2)}, u32[]{:S(2)}) collective-permute-start(f16[2,2,48,2048]{3,2,1,0:T(8,128)(2,1)S(1)} %fusion.5), channel_id=1, source_target_pairs={{0,8},{2,10},{4,12},{6,14},{8,0},{10,2},{12,4},{14,6},{16,24},{18,... | collective-permute-start | bytes 2359304 | tf_op jit(solution)/shard_map/ppermute | solution.py:21
  106.6 21.0 %collective-permute-start.6 = (f16[2,48,2048]{2,1,0:T(8,128)(2,1)S(1)}, f16[2,48,2048]{2,1,0:T(8,128)(2,1)S(1)}, u32[]{:S(2)}, u32[]{:S(2)}) collective-permute-start(f16[2,48,2048]{2,1,0:T(8,128)(2,1)S(1)} %get-tuple-element.66), channel_id=1, source_target_pairs={{0,8},{2,10},{4,12},{6,14},{8,0},{10,2},{12,4},{14,6},{16,24},{18,... | collective-permute-start | bytes 1179656 | tf_op jit(solution)/shard_map/ppermute | solution.py:21
  109.7 21.4 %collective-permute-start.14 = (f16[2,48,2048]{2,1,0:T(8,128)(2,1)S(1)}, f16[2,48,2048]{2,1,0:T(8,128)(2,1)S(1)}, u32[]{:S(2)}, u32[]{:S(2)}) collective-permute-start(f16[2,48,2048]{2,1,0:T(8,128)(2,1)S(1)} %get-tuple-element.64), channel_id=1, source_target_pairs={{0,4},{2,6},{4,0},{6,2},{8,12},{10,14},{12,8},{14,10},{16,20},{18,... | collective-permute-start | bytes 1179656 | tf_op jit(solution)/shard_map/ppermute | solution.py:21
  128.5 16.8 %collective-permute-start.13 = (f16[48,2048]{1,0:T(8,128)(2,1)S(1)}, f16[48,2048]{1,0:T(8,128)(2,1)S(1)}, u32[]{:S(2)}, u32[]{:S(2)}) collective-permute-start(f16[48,2048]{1,0:T(8,128)(2,1)S(1)} %get-tuple-element.98), channel_id=1, source_target_pairs={{0,16},{2,18},{4,20},{6,22},{8,24},{10,26},{12,28},{14,30},{16,0},... | collective-permute-start | bytes 589832 | tf_op jit(solution)/shard_map/ppermute | solution.py:21
  132.0 15.1 %collective-permute-start.15 = (f16[48,2048]{1,0:T(8,128)(2,1)S(1)}, f16[48,2048]{1,0:T(8,128)(2,1)S(1)}, u32[]{:S(2)}, u32[]{:S(2)}) collective-permute-start(f16[48,2048]{1,0:T(8,128)(2,1)S(1)} %get-tuple-element.96), channel_id=1, source_target_pairs={{0,16},{2,18},{4,20},{6,22},{8,24},{10,26},{12,28},{14,30},{16,0},... | collective-permute-start | bytes 589832 | tf_op jit(solution)/shard_map/ppermute | solution.py:21
  148.9 211.3 %all-gather.7.cloned.1.call-start = ((), (), s32[]{:S(2)}) async-start(), calls=%async_computation.1 | async-start | bytes 6684672 | tf_op jit(solution)/shard_map/all_gather | solution.py:262
  156.1 23.7 %collective-permute-start.20 = (f16[2,2,48,2048]{3,2,1,0:T(8,128)(2,1)S(1)}, f16[2,2,48,2048]{3,2,1,0:T(8,128)(2,1)S(1)}, u32[]{:S(2)}, u32[]{:S(2)}) collective-permute-start(f16[2,2,48,2048]{3,2,1,0:T(8,128)(2,1)S(1)} %bitcast.195), channel_id=1, source_target_pairs={{0,4},{2,6},{4,0},{6,2},{8,12},{10,14},{12,8},{14,10},{16,20},{18,... | collective-permute-start | bytes 2359304 | tf_op jit(solution)/shard_map/ppermute | solution.py:21
  161.9 33.5 %collective-permute-start.27 = (f16[2,2,48,2048]{3,2,1,0:T(8,128)(2,1)S(1)}, f16[2,2,48,2048]{3,2,1,0:T(8,128)(2,1)S(1)}, u32[]{:S(2)}, u32[]{:S(2)}) collective-permute-start(f16[2,2,48,2048]{3,2,1,0:T(8,128)(2,1)S(1)} %fusion.6), channel_id=1, source_target_pairs={{0,8},{2,10},{4,12},{6,14},{8,0},{10,2},{12,4},{14,6},{16,24},{18,... | collective-permute-start | bytes 2359304 | tf_op jit(solution)/shard_map/ppermute | solution.py:21
  181.0 33.7 %collective-permute-start.22 = (f16[2,48,2048]{2,1,0:T(8,128)(2,1)S(1)}, f16[2,48,2048]{2,1,0:T(8,128)(2,1)S(1)}, u32[]{:S(2)}, u32[]{:S(2)}) collective-permute-start(f16[2,48,2048]{2,1,0:T(8,128)(2,1)S(1)} %get-tuple-element.58), channel_id=1, source_target_pairs={{0,8},{2,10},{4,12},{6,14},{8,0},{10,2},{12,4},{14,6},{16,24},{18,... | collective-permute-start | bytes 1179656 | tf_op jit(solution)/shard_map/ppermute | solution.py:21
  196.8 19.1 %collective-permute-start.29 = (f16[2,48,2048]{2,1,0:T(8,128)(2,1)}, f16[2,48,2048]{2,1,0:T(8,128)(2,1)S(1)}, u32[]{:S(2)}, u32[]{:S(2)}) collective-permute-start(f16[2,48,2048]{2,1,0:T(8,128)(2,1)} %get-tuple-element.56), channel_id=1, source_target_pairs={{0,4},{2,6},{4,0},{6,2},{8,12},{10,14},{12,8},{14,10},{16,20},{18,... | collective-permute-start | bytes 1179656 | tf_op jit(solution)/shard_map/ppermute | solution.py:21
  215.7 22.7 %collective-permute-start.28 = (f16[48,2048]{1,0:T(8,128)(2,1)S(1)}, f16[48,2048]{1,0:T(8,128)(2,1)S(1)}, u32[]{:S(2)}, u32[]{:S(2)}) collective-permute-start(f16[48,2048]{1,0:T(8,128)(2,1)S(1)} %get-tuple-element.94), channel_id=1, source_target_pairs={{0,16},{2,18},{4,20},{6,22},{8,24},{10,26},{12,28},{14,30},{16,0},... | collective-permute-start | bytes 589832 | tf_op jit(solution)/shard_map/ppermute | solution.py:21
  216.8 25.7 %collective-permute-start.30 = (f16[48,2048]{1,0:T(8,128)(2,1)S(1)}, f16[48,2048]{1,0:T(8,128)(2,1)S(1)}, u32[]{:S(2)}, u32[]{:S(2)}) collective-permute-start(f16[48,2048]{1,0:T(8,128)(2,1)S(1)} %get-tuple-element.92), channel_id=1, source_target_pairs={{0,16},{2,18},{4,20},{6,22},{8,24},{10,26},{12,28},{14,30},{16,0},... | collective-permute-start | bytes 589832 | tf_op jit(solution)/shard_map/ppermute | solution.py:21
  253.1 16.0 %collective-permute-start.35 = (f16[2,2,32,2048]{3,2,1,0:T(8,128)(2,1)S(1)}, f16[2,2,32,2048]{3,2,1,0:T(8,128)(2,1)S(1)}, u32[]{:S(2)}, u32[]{:S(2)}) collective-permute-start(f16[2,2,32,2048]{3,2,1,0:T(8,128)(2,1)S(1)} %bitcast.196), channel_id=1, source_target_pairs={{0,4},{2,6},{4,0},{6,2},{8,12},{10,14},{12,8},{14,10},{16,20},{18,... | collective-permute-start | bytes 1572872 | tf_op jit(solution)/shard_map/ppermute | solution.py:21
  269.3 14.6 %collective-permute-start.36 = (f16[2,32,2048]{2,1,0:T(8,128)(2,1)S(1)}, f16[2,32,2048]{2,1,0:T(8,128)(2,1)S(1)}, u32[]{:S(2)}, u32[]{:S(2)}) collective-permute-start(f16[2,32,2048]{2,1,0:T(8,128)(2,1)S(1)} %fusion.26), channel_id=1, source_target_pairs={{0,8},{2,10},{4,12},{6,14},{8,0},{10,2},{12,4},{14,6},{16,24},{18,... | collective-permute-start | bytes 786440 | tf_op jit(solution)/shard_map/ppermute | solution.py:21
  269.8 44.0 %collective-permute-start.42 = (f16[2,2,32,2048]{3,2,1,0:T(8,128)(2,1)S(1)}, f16[2,2,32,2048]{3,2,1,0:T(8,128)(2,1)S(1)}, u32[]{:S(2)}, u32[]{:S(2)}) collective-permute-start(f16[2,2,32,2048]{3,2,1,0:T(8,128)(2,1)S(1)} %fusion.7), channel_id=1, source_target_pairs={{0,8},{2,10},{4,12},{6,14},{8,0},{10,2},{12,4},{14,6},{16,24},{18,... | collective-permute-start | bytes 1572872 | tf_op jit(solution)/shard_map/ppermute | solution.py:21
  314.1 9.4 %collective-permute-start.37 = (f16[32,2048]{1,0:T(8,128)(2,1)S(1)}, f16[32,2048]{1,0:T(8,128)(2,1)S(1)}, u32[]{:S(2)}, u32[]{:S(2)}) collective-permute-start(f16[32,2048]{1,0:T(8,128)(2,1)S(1)} %fusion.40), channel_id=1, source_target_pairs={{0,16},{2,18},{4,20},{6,22},{8,24},{10,26},{12,28},{14,30},{16,0},... | collective-permute-start | bytes 393224 | tf_op jit(solution)/shard_map/ppermute | solution.py:21
  320.5 8.0 %collective-permute-start.44 = (f16[32,2048]{1,0:T(8,128)(2,1)S(1)}, f16[32,2048]{1,0:T(8,128)(2,1)S(1)}, u32[]{:S(2)}, u32[]{:S(2)}) collective-permute-start(f16[32,2048]{1,0:T(8,128)(2,1)S(1)} %fusion.41), channel_id=1, source_target_pairs={{0,16},{2,18},{4,20},{6,22},{8,24},{10,26},{12,28},{14,30},{16,0},... | collective-permute-start | bytes 393224 | tf_op jit(solution)/shard_map/ppermute | solution.py:21
  331.9 7.9 %collective-permute-start.45 = (bf16[32,1024]{1,0:T(8,128)(2,1)S(1)}, bf16[32,1024]{1,0:T(8,128)(2,1)S(1)}, u32[]{:S(2)}, u32[]{:S(2)}) collective-permute-start(bf16[32,1024]{1,0:T(8,128)(2,1)S(1)} %get-tuple-element.121), channel_id=1, source_target_pairs={{0,16},{2,18},{4,20},{6,22},{8,24},{10,26},{12,28},{14,30},{16,0},... | collective-permute-start | bytes 196616 | tf_op jit(solution)/shard_map/ppermute | solution.py:21
  334.8 8.2 %collective-permute-start.58 = (bf16[2,32,1024]{2,1,0:T(8,128)(2,1)S(1)}, bf16[2,32,1024]{2,1,0:T(8,128)(2,1)S(1)}, u32[]{:S(2)}, u32[]{:S(2)}) collective-permute-start(bf16[2,32,1024]{2,1,0:T(8,128)(2,1)S(1)} %get-tuple-element.109), channel_id=1, source_target_pairs={{0,4},{2,6},{4,0},{6,2},{8,12},{10,14},{12,8},{14,10},{16,20},{18,... | collective-permute-start | bytes 393224 | tf_op jit(solution)/shard_map/ppermute | solution.py:21
  335.0 13.4 %collective-permute-start.54 = (bf16[2,32,1024]{2,1,0:T(8,128)(2,1)S(1)}, bf16[2,32,1024]{2,1,0:T(8,128)(2,1)S(1)}, u32[]{:S(2)}, u32[]{:S(2)}) collective-permute-start(bf16[2,32,1024]{2,1,0:T(8,128)(2,1)S(1)} %get-tuple-element.115), channel_id=1, source_target_pairs={{0,8},{2,10},{4,12},{6,14},{8,0},{10,2},{12,4},{14,6},{16,24},{18,... | collective-permute-start | bytes 393224 | tf_op jit(solution)/shard_map/ppermute | solution.py:21
  343.0 7.9 %collective-permute-start.59 = (bf16[2,2,32,1024]{3,2,1,0:T(8,128)(2,1)S(1)}, bf16[2,2,32,1024]{3,2,1,0:T(8,128)(2,1)S(1)}, u32[]{:S(2)}, u32[]{:S(2)}) collective-permute-start(bf16[2,2,32,1024]{3,2,1,0:T(8,128)(2,1)S(1)} %get-tuple-element.101), channel_id=1, source_target_pairs={{0,8},{2,10},{4,12},{6,14},{8,0},{10,2},{12,4},{14,6},{16,24},{18,... | collective-permute-start | bytes 786440 | tf_op jit(solution)/shard_map/ppermute | solution.py:21
  345.4 8.4 %collective-permute-start.51 = (bf16[2,2,32,1024]{3,2,1,0:T(8,128)(2,1)S(1)}, bf16[2,2,32,1024]{3,2,1,0:T(8,128)(2,1)S(1)}, u32[]{:S(2)}, u32[]{:S(2)}) collective-permute-start(bf16[2,2,32,1024]{3,2,1,0:T(8,128)(2,1)S(1)} %get-tuple-element.105), channel_id=1, source_target_pairs={{0,8},{2,10},{4,12},{6,14},{8,0},{10,2},{12,4},{14,6},{16,24},{18,... | collective-permute-start | bytes 786440 | tf_op jit(solution)/shard_map/ppermute | solution.py:21
  348.4 8.2 %collective-permute-start.55 = (bf16[2,2,32,1024]{3,2,1,0:T(8,128)(2,1)S(1)}, bf16[2,2,32,1024]{3,2,1,0:T(8,128)(2,1)S(1)}, u32[]{:S(2)}, u32[]{:S(2)}) collective-permute-start(bf16[2,2,32,1024]{3,2,1,0:T(8,128)(2,1)S(1)} %get-tuple-element.103), channel_id=1, source_target_pairs={{0,4},{2,6},{4,0},{6,2},{8,12},{10,14},{12,8},{14,10},{16,20},{18,... | collective-permute-start | bytes 786440 | tf_op jit(solution)/shard_map/ppermute | solution.py:21
  (58 other events, 246.8 us)
Sparse Core Ops, SparseCore 0:
  149.0 90.9 all-gather.4
  245.1 70.7 all-gather.6
